TPU v7x, 256 devices: a whole 4x4x8 slice. The times are simulated.
256 devices in a mesh: batch: 256 (over z, x, y, core).
Axes of the slice: x: 4, y: 4, z: 8, core: 2. Of those that a mesh axis runs over, the one named last changes fastest.
Arguments:
- img_emb: bfloat16 [131072, 1152], P('batch'), may hold values from -0.19921875 to 0.19921875
- txt_feat: bfloat16 [131072, 1152], P('batch'), may hold values from -0.19921875 to 0.19921875
- txt_head: bfloat16 [1152, 1152], replicated, may hold values from -0.1875 to 0.1875
- log_scale: float32 [1], replicated, may hold values from 1 to 2.3
- bias: float32 [1], replicated, may hold values from -4 to -1
Outputs:
- img_grad: bfloat16 [131072, 1152], P('batch')
- txt_grad: bfloat16 [131072, 1152], P('batch')
- head_grad: float32 [1152, 1152], replicated
All inputs are finite; a program needn't handle non-finite values.
Results may differ from a plain program's by a relative error of at most 0.0067.
Values may be sent and summed in bfloat16 or wider, within the bound.
A program may use at most 64 MiB of HBM per device.

v0:
```python
import jax
import jax.numpy as jnp
from jax import lax
from jax.sharding import PartitionSpec as P


def passed_along(block, axis, distance):
    devices = range(lax.axis_size(axis))
    route = [((i - distance) % len(devices), i) for i in devices]
    return lax.ppermute(block, axis, route)


def unit_rows(values):
    rinv = lax.rsqrt(jnp.sum(values * values, axis=-1, keepdims=True) + 1e-06)
    return (values * rinv, rinv)


def pair_weights(images, texts, scale, offset, diag_at):
    logits = (
        scale
        * lax.dot_general(
            images, texts, (((1,), (1,)), ((), ())), preferred_element_type=jnp.float32
        )
        + offset
    )
    shape = (images.shape[0], texts.shape[0])
    row_id = lax.broadcasted_iota(jnp.int32, shape, 0)
    col_id = lax.broadcasted_iota(jnp.int32, shape, 1)
    sign = jnp.where(col_id == row_id + diag_at, jnp.float32(1.0), jnp.float32(-1.0))
    grads = sign * (jax.nn.sigmoid(sign * logits) - 1.0)
    return (scale * grads).astype(jnp.bfloat16)


def image_terms(weight, images):
    return lax.dot_general(
        weight, images, (((0,), (0,)), ((), ())), preferred_element_type=jnp.float32
    )


def fetch_left(unit_txt):
    return passed_along(unit_txt, "batch", 1)


def return_left(part):
    return passed_along(part, "batch", -1)


def return_right(part):
    return passed_along(part, "batch", 1)


def shards(img_emb, txt_feat, txt_head, log_scale, bias):
    rows = img_emb.shape[0]
    scale = jnp.exp(log_scale[0])
    offset = bias[0]
    img_unit, img_rinv = unit_rows(img_emb.astype(jnp.float32))
    hidden = jnp.dot(txt_feat, txt_head, preferred_element_type=jnp.float32)
    txt_unit, txt_rinv = unit_rows(hidden)
    unit_img = img_unit.astype(jnp.bfloat16)
    unit_txt = txt_unit.astype(jnp.bfloat16)
    weight_own = pair_weights(unit_img, unit_txt, scale, offset, 0)
    unit_grad = jnp.dot(weight_own, unit_txt, preferred_element_type=jnp.float32)
    part_own = image_terms(weight_own, unit_img)
    left_txt = fetch_left(unit_txt)
    weight_left = pair_weights(unit_img, left_txt, scale, offset, rows)
    unit_grad = unit_grad + jnp.dot(weight_left, left_txt, preferred_element_type=jnp.float32)
    part_left = image_terms(weight_left, unit_img).astype(jnp.bfloat16)
    back_left = return_left(part_left)
    right_txt = passed_along(unit_txt, "batch", -1)
    weight_right = pair_weights(unit_img, right_txt, scale, offset, rows)
    unit_grad = unit_grad + jnp.dot(weight_right, right_txt, preferred_element_type=jnp.float32)
    back_right = return_right(image_terms(weight_right, unit_img).astype(jnp.bfloat16))
    text_unit_grad = part_own + back_left.astype(jnp.float32) + back_right.astype(jnp.float32)
    img_grad = (
        unit_grad - img_unit * jnp.sum(img_unit * unit_grad, axis=-1, keepdims=True)
    ) * img_rinv
    hidden_grad = (
        text_unit_grad - txt_unit * jnp.sum(txt_unit * text_unit_grad, axis=-1, keepdims=True)
    ) * txt_rinv
    hidden_grad = hidden_grad.astype(jnp.bfloat16)
    txt_grad = lax.dot_general(
        hidden_grad, txt_head, (((1,), (1,)), ((), ())), preferred_element_type=jnp.float32
    )
    head_local = lax.dot_general(
        txt_feat, hidden_grad, (((0,), (0,)), ((), ())), preferred_element_type=jnp.float32
    )
    head_grad = lax.psum(head_local, "batch")
    return (img_grad.astype(jnp.bfloat16), txt_grad.astype(jnp.bfloat16), head_grad)


def solution(mesh):
    return jax.shard_map(
        shards,
        mesh=mesh,
        in_specs=(P("batch", None), P("batch", None), P(), P(), P()),
        out_specs=(P("batch", None), P("batch", None), P()),
        check_vma=False,
    )
```

profile of v0, /device:TPU:1, one launch (start us, length us, event | category | flops | bytes accessed | tf_op | source)
XLA Modules:
  0.0 352.8 jit_solution(8681824240222110929)
XLA Ops:
  7.2 1.7 copy-done
  8.9 3.2 multiply_reduce_fusion.1
  12.4 3.3 collective-permute-start.1
  17.4 11.7 %collective-permute-done.1 = bf16[512,1152]{1,0:T(8,128)(2,1)S(1)} collective-permute-done((bf16[512,1152]{1,0:T(8,128)(2,1)S(1)}, bf16[512,1152]{1,0:T(8,128)(2,1)S(1)}, u32[]{:S(2)}, u32[]{:S(2)}) %collective-permute-start.1) | collective-permute-done | bytes 1179680 | tf_op jit(solution)/shard_map/ppermute | solution.py:10
  29.0 1.2 fusion.31
  30.3 0.9 convolution_convert_fusion.1
  31.3 1.2 fusion.27
  32.6 1.0 convolution_convert_fusion.2
  33.6 13.9 %collective-permute-start.2 = (bf16[512,1152]{1,0:T(8,128)(2,1)S(1)}, bf16[512,1152]{1,0:T(8,128)(2,1)S(1)}, u32[]{:S(2)}, u32[]{:S(2)}) collective-permute-start(bf16[512,1152]{1,0:T(8,128)(2,1)S(1)} %convolution_convert_fusion.2), channel_id=1, source_target_pairs={{1,0},{2,1},{3,2},{4,3},{5,4},{6,5},{7,6},{8,7},{9,8},{10,9},{11,1... | collective-permute-start | bytes 3538952 | tf_op jit(solution)/shard_map/ppermute | solution.py:10
  47.5 1.1 fusion.23
  48.6 1.4 collective-permute-done.2
  50.0 1.4 multiply_reduce_fusion
  51.4 0.7 multiply_convert_fusion
  52.1 1.0 copy-done.3
  53.1 4.1 %convolution_bitcast_fusion = f32[1152,1152]{0,1:T(8,128)} fusion(bf16[512,1152]{1,0:T(8,128)(2,1)S(1)} %multiply_convert_fusion, bf16[512,1152]{1,0:T(8,128)(2,1)S(1)} %copy-done.8), kind=kOutput, calls=%fused_computation | convolution fusion | flops 1358954496 | bytes 7667712 | tf_op jit(solution)/shard_map/dot_general | solution.py:84
  57.3 2.2 fusion.39
  59.5 0.9 convolution_add_fusion.1
  60.4 0.4 copy-done.2
  60.8 0.4 copy-done.7
  61.3 1.1 fusion.3
  62.4 1.5 fusion.6
  63.9 2.9 convolution_convert_fusion
  66.8 272.3 %all-reduce.2.cloned.1.call-done = f32[1152,1152]{0,1:T(8,128)} async-done(((f32[1152,1152]{0,1:T(8,128)}), f32[1152,1152]{0,1:T(8,128)}) %all-reduce.2.cloned.1.call-update) | async-done | bytes 5308432 | tf_op jit(solution)/shard_map/psum | solution.py:87
  339.1 6.9 %copy.8 = f32[1152,1152]{1,0:T(8,128)} copy(f32[1152,1152]{0,1:T(8,128)} %all-reduce.2.cloned.1.call-done) | data formatting | bytes 10616832
  (37 shorter events, 0.9 us)
Async XLA Ops:
  7.2 1.8 copy-start
  7.2 332.0 %all-reduce.2.cloned.1.call-start = ((), (), s32[]{:S(2)}) async-start(), calls=%async_computation | async-start | bytes 10616832 | tf_op jit(solution)/shard_map/psum | solution.py:87
  12.1 4.9 %copy-start.1 = (bf16[512,1152]{1,0:T(8,128)(2,1)S(1)}, bf16[512,1152]{1,0:T(8,128)(2,1)}, u32[]{:S(2)}) copy-start(bf16[512,1152]{1,0:T(8,128)(2,1)} %param.5) | copy-start | bytes 3538948
  12.4 35.1 %copy-start.5 = (bf16[512,1152]{1,0:T(8,128)(2,1)}, bf16[512,1152]{1,0:T(8,128)(2,1)S(1)}, u32[]{:S(2)}) copy-start(bf16[512,1152]{1,0:T(8,128)(2,1)S(1)} %multiply_convert_fusion.1) | copy-start | bytes 3538948
  12.4 16.7 %collective-permute-start.1 = (bf16[512,1152]{1,0:T(8,128)(2,1)S(1)}, bf16[512,1152]{1,0:T(8,128)(2,1)S(1)}, u32[]{:S(2)}, u32[]{:S(2)}) collective-permute-start(bf16[512,1152]{1,0:T(8,128)(2,1)S(1)} %multiply_convert_fusion.1), channel_id=1, source_target_pairs={{1,0},{2,1},{3,2},{4,3},{5,4},{6,5},{7,6},{8,7},{9,8},{10,9},{11,1... | collective-permute-start | bytes 3538952 | tf_op jit(solution)/shard_map/ppermute | solution.py:10
  15.7 15.6 %collective-permute-start = (bf16[512,1152]{1,0:T(8,128)(2,1)S(1)}, bf16[512,1152]{1,0:T(8,128)(2,1)S(1)}, u32[]{:S(2)}, u32[]{:S(2)}) collective-permute-start(bf16[512,1152]{1,0:T(8,128)(2,1)S(1)} %multiply_convert_fusion.1), channel_id=1, source_target_pairs={{255,0},{0,1},{1,2},{2,3},{3,4},{4,5},{5,6},{6,7},{7,8},{8,9},{9,1... | collective-permute-start | bytes 3538952 | tf_op jit(solution)/shard_map/ppermute | solution.py:10
  29.0 1.2 copy-start.6
  30.3 2.3 copy-start.11
  31.2 17.4 %collective-permute-start.3 = (bf16[512,1152]{1,0:T(8,128)(2,1)S(1)}, bf16[512,1152]{1,0:T(8,128)(2,1)S(1)}, u32[]{:S(2)}, u32[]{:S(2)}) collective-permute-start(bf16[512,1152]{1,0:T(8,128)(2,1)S(1)} %convolution_convert_fusion.1), channel_id=1, source_target_pairs={{255,0},{0,1},{1,2},{2,3},{3,4},{4,5},{5,6},{6,7},{7,8},{8,9},{9,1... | collective-permute-start | bytes 3538952 | tf_op jit(solution)/shard_map/ppermute | solution.py:10
  31.3 1.3 copy-start.9
  32.6 16.0 %copy-start.13 = (bf16[512,512]{1,0:T(8,128)(2,1)}, bf16[512,512]{1,0:T(8,128)(2,1)S(1)}, u32[]{:S(2)}) copy-start(bf16[512,512]{1,0:T(8,128)(2,1)S(1)} %fusion.27) | copy-start | bytes 1572868
  33.6 16.4 %collective-permute-start.2 = (bf16[512,1152]{1,0:T(8,128)(2,1)S(1)}, bf16[512,1152]{1,0:T(8,128)(2,1)S(1)}, u32[]{:S(2)}, u32[]{:S(2)}) collective-permute-start(bf16[512,1152]{1,0:T(8,128)(2,1)S(1)} %convolution_convert_fusion.2), channel_id=1, source_target_pairs={{1,0},{2,1},{3,2},{4,3},{5,4},{6,5},{7,6},{8,7},{9,8},{10,9},{11,1... | collective-permute-start | bytes 3538952 | tf_op jit(solution)/shard_map/ppermute | solution.py:10
  51.4 1.7 copy-start.8
  52.1 1.0 copy-start.3
  57.2 2.3 copy-start.10
  57.2 2.3 copy-start.14
  59.5 1.3 copy-start.2
  59.5 1.6 copy-start.7
  59.5 1.7 copy-start.12
  62.4 1.5 copy-start.4
Sparse Core Ops, SparseCore 0:
  57.4 281.7 all-reduce.1
where the time goes:
time: 354 us; the launch traced here: 353 us
  waiting for transfers between devices  285 us (81%)
  matrix products  21.4 us (6%)
  starting transfers between devices  17.3 us (5%)
  between operations  15.6 us (4%)
  local copies, waits for them, and re-layouts  10.5 us (3%)
    psum x1, waiting for transfers between devices, shards(): head_grad = lax.psum(head_local, 'batch')  272 us
    ppermute x4, starting transfers between devices, passed_along(): return lax.ppermute(block, axis, route)  17.3 us
    ppermute x4, waiting for transfers between devices, passed_along(): return lax.ppermute(block, axis, route)  13 us
    unnamed x31, local copies, waits for them, and re-layouts  10.5 us
  transfers between devices with their start and end apart: 5, of which 3 were waited for; matrix products, arithmetic and copies ran while one was open for 4% of the time, Pallas kernels for 0%

commit v1 on v0

--- a/solution.py
+++ b/solution.py
@@ -1,7 +1,306 @@
+import functools
+
 import jax
 import jax.numpy as jnp
 from jax import lax
+from jax.experimental import pallas as pl
+from jax.experimental.pallas import tpu as pltpu
 from jax.sharding import PartitionSpec as P
+
+MESH = pl.DeviceIdType.MESH
+F32 = jnp.float32
+BF16 = jnp.bfloat16
+ZS, XS, YS, CS = 8, 4, 4, 2
+XY = XS * YS
+E = 1152
+ROWS = 512
+HALF = E // 2
+COLS = E // 128
+UNITS = HALF // 16
+PA = 14
+PB = 13
+NA = PA * XY
+NB = PB * ZS
+NT = NA + NB
+
+
+def coords(me):
+    return (me // (XS * YS * CS), (me // (YS * CS)) % XS, (me // CS) % YS, me % CS)
+
+
+def device(z, x, y, c):
+    return ((z * XS + x) * YS + y) * CS + c
+
+
+def xy_member(me, d):
+    z, x, y, c = coords(me)
+    x = (x + d // YS) % XS
+    y = (y + d % YS) % YS
+    return (device(z, x, y, c), x * YS + y)
+
+
+def xy_source(me, d):
+    z, x, y, c = coords(me)
+    return ((x + XS - d // YS) % XS) * YS + (y + YS - d % YS) % YS
+
+
+def z_member(me, d):
+    z, x, y, c = coords(me)
+    z = (z + d) % ZS
+    return (device(z, x, y, c), z)
+
+
+def other_core(me):
+    return me + 1 - 2 * (me % CS)
+
+
+def remote(src, dst, ssem, rsem, to):
+    return pltpu.make_async_remote_copy(
+        src_ref=src, dst_ref=dst, send_sem=ssem, recv_sem=rsem,
+        device_id=(to,), device_id_type=MESH,
+    )
+
+
+def each(lo, hi, body):
+    def step(i, carry):
+        body(i)
+        return carry
+
+    lax.fori_loop(lo, hi, step, 0)
+
+
+def all_reduce(me, w, out, s):
+    z, x, y, c = coords(me)
+    p = x * YS + y
+    nbr = other_core(me)
+
+    def a1(d):
+        to, q = xy_member(me, d)
+        return remote(w.at[pl.ds(q * PA, PA)], s.ra1.at[d], s.s1.at[d], s.r1.at[d], to)
+
+    def b1(d):
+        to, q = z_member(me, d)
+        return remote(w.at[pl.ds(NA + q * PB, PB)], s.rb1.at[d], s.s1.at[XY + d], s.r1.at[XY + d], to)
+
+    def a2(d):
+        to, q = z_member(me, d)
+        return remote(s.sa.at[pl.ds(q * 2, 2)], s.ra2.at[d], s.s2.at[XY + d], s.r2.at[XY + d], to)
+
+    def b2(d):
+        to, q = xy_member(me, d)
+        return remote(s.sb.at[pl.ds(q, 1)], s.rb2.at[d], s.s2.at[d], s.r2.at[d], to)
+
+    def a3(d):
+        to, q = z_member(me, d)
+        here = s.ga.at[pl.ds(z * 2, 2)]
+        return remote(here, here, s.s3.at[XY + d], s.r3.at[XY + d], to)
+
+    def b3(d):
+        to, q = xy_member(me, d)
+        here = s.gb.at[pl.ds(p, 1)]
+        return remote(here, here, s.s3.at[d], s.r3.at[d], to)
+
+    def a4(d):
+        to, q = xy_member(me, d)
+        return remote(s.ga.at[pl.ds(0, PA)], out.at[c, pl.ds(p * PA, PA)], s.s4.at[d], s.r4.at[d], to)
+
+    def b4(d):
+        to, q = z_member(me, d)
+        return remote(s.gb.at[pl.ds(0, PB)], out.at[c, pl.ds(NA + z * PB, PB)], s.s4.at[XY + d], s.r4.at[XY + d], to)
+
+    def fa(d):
+        q = xy_source(me, d)
+        here = out.at[c, pl.ds(q * PA, PA)]
+        return remote(here, here, s.s5.at[d], s.r5.at[d], nbr)
+
+    def fb(d):
+        q = z_member(me, ZS - d)[1]
+        here = out.at[c, pl.ds(NA + q * PB, PB)]
+        return remote(here, here, s.s5.at[XY + d], s.r5.at[XY + d], nbr)
+
+    each(1, ZS, lambda d: b1(d).start())
+    each(1, XY, lambda d: a1(d).start())
+    each(1, ZS, lambda d: b1(d).wait_recv())
+
+    def sum_b1(i):
+        total = w[NA + z * PB + i].astype(F32) + jnp.sum(s.rb1[1:, i].astype(F32), axis=0)
+        s.sb[i] = total.astype(BF16)
+
+    each(0, PB, sum_b1)
+    s.sb[PB:] = jnp.zeros((XY - PB, 16, 128), BF16)
+    each(1, XY, lambda d: b2(d).start())
+    each(1, XY, lambda d: a1(d).wait_recv())
+
+    def sum_a1(i):
+        total = w[p * PA + i].astype(F32) + jnp.sum(s.ra1[1:, i].astype(F32), axis=0)
+        s.sa[i] = total.astype(BF16)
+
+    each(0, PA, sum_a1)
+    s.sa[PA:] = jnp.zeros((2 * ZS - PA, 16, 128), BF16)
+    each(1, ZS, lambda d: a2(d).start())
+    each(1, XY, lambda d: b2(d).wait_recv())
+    total = s.sb[p].astype(F32) + jnp.sum(s.rb2[1:, 0].astype(F32), axis=0)
+    s.gb[p] = total.astype(BF16)
+    each(1, XY, lambda d: b3(d).start())
+    each(1, ZS, lambda d: a2(d).wait_recv())
+
+    def sum_a2(i):
+        total = s.sa[z * 2 + i].astype(F32) + jnp.sum(s.ra2[1:, i].astype(F32), axis=0)
+        s.ga[z * 2 + i] = total.astype(BF16)
+
+    each(0, 2, sum_a2)
+    each(1, ZS, lambda d: a3(d).start())
+    each(1, XY, lambda d: b3(d).wait_recv())
+    each(1, ZS, lambda d: b4(d).start())
+    own_b = pltpu.make_async_copy(s.gb.at[pl.ds(0, PB)], out.at[c, pl.ds(NA + z * PB, PB)], s.own.at[0])
+    own_b.start()
+    each(1, ZS, lambda d: a3(d).wait_recv())
+    each(1, XY, lambda d: a4(d).start())
+    own_a = pltpu.make_async_copy(s.ga.at[pl.ds(0, PA)], out.at[c, pl.ds(p * PA, PA)], s.own.at[1])
+    own_a.start()
+    own_b.wait()
+    own_a.wait()
+    fb(0).start()
+    fa(0).start()
+
+    def pass_b(d):
+        b4(d).wait_recv()
+        fb(d).start()
+
+    def pass_a(d):
+        a4(d).wait_recv()
+        fa(d).start()
+
+    each(1, ZS, pass_b)
+    each(1, XY, pass_a)
+    for first, last in ((a1, b1), (b2, a2), (b3, a3), (a4, b4)):
+        each(1, XY, lambda d: first(d).wait_send())
+        each(1, ZS, lambda d: last(d).wait_send())
+    each(0, XY, lambda d: fa(d).wait())
+    each(0, ZS, lambda d: fb(d).wait())
+
+
+class Names:
+    pass
+
+
+AR_SCRATCH = dict(
+    ra1=pltpu.VMEM((XY, PA, 16, 128), BF16),
+    rb1=pltpu.VMEM((ZS, PB, 16, 128), BF16),
+    sa=pltpu.VMEM((2 * ZS, 16, 128), BF16),
+    sb=pltpu.VMEM((XY, 16, 128), BF16),
+    ra2=pltpu.VMEM((ZS, 2, 16, 128), BF16),
+    rb2=pltpu.VMEM((XY, 1, 16, 128), BF16),
+    ga=pltpu.VMEM((2 * ZS, 16, 128), BF16),
+    gb=pltpu.VMEM((XY, 16, 128), BF16),
+    s1=pltpu.SemaphoreType.DMA((XY + ZS,)),
+    r1=pltpu.SemaphoreType.DMA((XY + ZS,)),
+    s2=pltpu.SemaphoreType.DMA((XY + ZS,)),
+    r2=pltpu.SemaphoreType.DMA((XY + ZS,)),
+    s3=pltpu.SemaphoreType.DMA((XY + ZS,)),
+    r3=pltpu.SemaphoreType.DMA((XY + ZS,)),
+    s4=pltpu.SemaphoreType.DMA((XY + ZS,)),
+    r4=pltpu.SemaphoreType.DMA((XY + ZS,)),
+    s5=pltpu.SemaphoreType.DMA((XY + ZS,)),
+    r5=pltpu.SemaphoreType.DMA((XY + ZS,)),
+    own=pltpu.SemaphoreType.DMA((2,)),
+)
+
+
+def enter(me):
+    barrier = pltpu.get_barrier_semaphore()
+
+    def greet(to):
+        pl.semaphore_signal(barrier, inc=1, device_id=(to,), device_id_type=MESH)
+
+    greet(other_core(me))
+    each(1, XY, lambda d: greet(xy_member(me, d)[0]))
+    each(1, ZS, lambda d: greet(z_member(me, d)[0]))
+    pl.semaphore_wait(barrier, XY + ZS - 1)
+
+
+def head_kernel(txt_ref, hid_ref, out, *scratch):
+    me = lax.axis_index("batch")
+    c = me % CS
+    s = Names()
+    for name, ref in zip(list(HEAD_SCRATCH), scratch):
+        setattr(s, name, ref)
+    enter(me)
+    nbr = other_core(me)
+    theirs = pl.ds(pl.multiple_of((1 - c) * HALF, HALF), HALF)
+    hid_copy = remote(hid_ref, s.hid_nbr, s.cs.at[1], s.cr.at[1], nbr)
+    hid_copy.start()
+
+    def flip(i):
+        cols = pl.ds(pl.multiple_of(i * 128, 128), 128)
+        s.txt_t[cols, :] = txt_ref[:, cols].T
+
+    each(0, COLS, flip)
+    txt_copy = remote(s.txt_t.at[theirs], s.txt_nbr, s.cs.at[0], s.cr.at[0], nbr)
+    txt_copy.start()
+    txt_copy.wait_recv()
+    hid_copy.wait_recv()
+    step = 6
+
+    def rows_of(i):
+        at = pl.multiple_of(i * 16 * step, 16 * step)
+        mine = s.txt_t[pl.ds(pl.multiple_of(c * HALF + at, 16 * step), 16 * step), :]
+        value = jnp.dot(mine, hid_ref[...], preferred_element_type=F32)
+        value += jnp.dot(s.txt_nbr[pl.ds(at, 16 * step), :], s.hid_nbr[...], preferred_element_type=F32)
+        value = value.astype(BF16)
+        for r in range(step):
+            for col in range(COLS):
+                s.w[(i * step + r) * COLS + col] = value[r * 16:(r + 1) * 16, col * 128:(col + 1) * 128]
+
+    each(0, UNITS // step, rows_of)
+    s.w[UNITS * COLS:] = jnp.zeros((NT - UNITS * COLS, 16, 128), BF16)
+    all_reduce(me, s.w, out, s)
+    txt_copy.wait_send()
+    hid_copy.wait_send()
+
+
+HEAD_SCRATCH = dict(
+    w=pltpu.VMEM((NT, 16, 128), BF16),
+    txt_t=pltpu.VMEM((E, ROWS), BF16),
+    txt_nbr=pltpu.VMEM((HALF, ROWS), BF16),
+    hid_nbr=pltpu.VMEM((ROWS, E), BF16),
+    cs=pltpu.SemaphoreType.DMA((2,)),
+    cr=pltpu.SemaphoreType.DMA((2,)),
+    **AR_SCRATCH,
+)
+
+
+def head_tiles(txt_feat, hidden_grad):
+    return pl.pallas_call(
+        head_kernel,
+        out_shape=jax.ShapeDtypeStruct((CS, NT, 16, 128), BF16),
+        in_specs=[pl.BlockSpec(memory_space=pltpu.VMEM)] * 2,
+        out_specs=pl.BlockSpec(memory_space=pl.ANY),
+        scratch_shapes=list(HEAD_SCRATCH.values()),
+        compiler_params=pltpu.CompilerParams(
+            collective_id=0, has_side_effects=True, vmem_limit_bytes=48 << 20
+        ),
+        name="head",
+    )(txt_feat, hidden_grad)
+
+
+def lay_kernel(step, tiles_ref, out_ref):
+    for r in range(step):
+        for col in range(COLS):
+            out_ref[r * 16:(r + 1) * 16, col * 128:(col + 1) * 128] = tiles_ref[r * COLS + col].astype(F32)
+
+
+def lay_out(tiles):
+    step = 6
+    blocks = UNITS // step
+    return pl.pallas_call(
+        functools.partial(lay_kernel, step),
+        out_shape=jax.ShapeDtypeStruct((E, E), F32),
+        grid=(CS * blocks,),
+        in_specs=[pl.BlockSpec((None, step * COLS, 16, 128), lambda i: (i // blocks, i % blocks, 0, 0))],
+        out_specs=pl.BlockSpec((step * 16, E), lambda i: (i, 0)),
+        name="lay_out",
+    )(tiles)
 
 
 def passed_along(block, axis, distance):
@@ -81,10 +380,7 @@
     txt_grad = lax.dot_general(
         hidden_grad, txt_head, (((1,), (1,)), ((), ())), preferred_element_type=jnp.float32
     )
-    head_local = lax.dot_general(
-        txt_feat, hidden_grad, (((0,), (0,)), ((), ())), preferred_element_type=jnp.float32
-    )
-    head_grad = lax.psum(head_local, "batch")
+    head_grad = lay_out(head_tiles(txt_feat, hidden_grad))
     return (img_grad.astype(jnp.bfloat16), txt_grad.astype(jnp.bfloat16), head_grad)
 
 

time: 354 us -> 122 us (0.34)
  waiting for transfers between devices: 285 us -> 17.4 us
  Pallas kernels: 0 us -> 69.9 us
  between operations: 15.6 us -> 2.11 us
  local copies, waits for them, and re-layouts: 10.5 us -> 3.28 us
  starting transfers between devices: 17.3 us -> 10.4 us
  matrix products: 21.4 us -> 15.7 us
    psum x1 -> x0, waiting for transfers between devices: 272 us -> none  [shards(): head_grad = lax.psum(head_local, 'batch')]
    pallas_call x0 -> x2, Pallas kernels: none -> 69.9 us  [the longest x1 61.6 us: head_tiles(): pl.pallas_call(head_kernel, out_shape=jax.ShapeDtypeStruct((CS, NT, 16, 1...]
    unnamed x31 -> x8, local copies, waits for them, and re-layouts: 10.5 us -> 3.28 us
    ppermute x4, starting transfers between devices: 17.3 us -> 10.4 us  [passed_along(): return lax.ppermute(block, axis, route)]
    ppermute x4, waiting for transfers between devices: 13 us -> 17.4 us  [passed_along(): return lax.ppermute(block, axis, route)]
    dot_general x1 -> x0, matrix products: 4.12 us -> none  [shards(): lax.dot_general(txt_feat, hidden_grad, (((0,), (0,)), ((), ())), preferre...]
  transfers between devices with their start and end apart: 5 -> 4, of which waited for: 3 -> 3; matrix products, arithmetic and copies ran while one was open for 4% -> 8% of each run, Pallas kernels for 0% -> 0%
where the time goes in v1:
time: 122 us
  Pallas kernels  69.9 us (57%)
  waiting for transfers between devices  17.4 us (14%)
  matrix products  15.7 us (13%)
  starting transfers between devices  10.4 us (9%)
  local copies, waits for them, and re-layouts  3.28 us (3%)
  other arithmetic  2.76 us (2%)
  between operations  2.11 us (2%)
    pallas_call x1, Pallas kernels, head_tiles(): pl.pallas_call(head_kernel, out_shape=jax.ShapeDtypeStruct((CS, NT, 16, 1...  61.6 us
    ppermute x4, waiting for transfers between devices, passed_along(): return lax.ppermute(block, axis, route)  17.4 us
    ppermute x4, starting transfers between devices, passed_along(): return lax.ppermute(block, axis, route)  10.4 us
    pallas_call x1, Pallas kernels, lay_out(): pl.pallas_call(functools.partial(lay_kernel, step), out_shape=jax.ShapeDt...  8.26 us
    dot_general x3, matrix products, pair_weights(): lax.dot_general(images, texts, (((1,), (1,)), ((), ())), preferred_elemen...  3.58 us
    unnamed x8, local copies, waits for them, and re-layouts  3.28 us
    dot_general x3, matrix products, image_terms(): lax.dot_general(weight, images, (((0,), (0,)), ((), ())), preferred_eleme...  3.26 us
    dot_general x1, matrix products, shards(): hidden = jnp.dot(txt_feat, txt_head, preferred_element_type=jnp.float32)  3.2 us
  transfers between devices with their start and end apart: 4, of which 3 were waited for; matrix products, arithmetic and copies ran while one was open for 8% of the time, Pallas kernels for 0%

profile of v1, /device:TPU:1, one launch (start us, length us, event | category | flops | bytes accessed | tf_op | source)
XLA Modules:
  0.0 121.6 jit_solution(11623335443433690628)
XLA Ops:
  0.6 1.7 %copy-done = bf16[1152,1152]{1,0:T(8,128)(2,1)S(1)} copy-done((bf16[1152,1152]{1,0:T(8,128)(2,1)S(1)}, bf16[1152,1152]{1,0:T(8,128)(2,1)}, u32[]{:S(2)}) %copy-start) | copy-done | bytes 2654232
  2.4 3.2 %multiply_reduce_fusion.1 = (f32[512]{0:T(512)S(1)}, f32[512,1152]{1,0:T(8,128)S(1)}) fusion(bf16[512,1152]{1,0:T(8,128)(2,1)} %txt_ref.1, bf16[1152,1152]{1,0:T(8,128)(2,1)S(1)} %copy-done), kind=kOutput, calls=%fused_computation.18 | convolution fusion | flops 1360133632 | bytes 6195200 | tf_op jit(solution)/shard_map/dot_general | solution.py:356
  5.8 2.8 %collective-permute-start = (bf16[512,1152]{1,0:T(8,128)(2,1)S(1)}, bf16[512,1152]{1,0:T(8,128)(2,1)S(1)}, u32[]{:S(2)}, u32[]{:S(2)}) collective-permute-start(bf16[512,1152]{1,0:T(8,128)(2,1)S(1)} %multiply_convert_fusion.1), channel_id=1, source_target_pairs={{255,0},{0,1},{1,2},{2,3},{3,4},{4,5},{5,6},{6,7},{7,8},{8,9},{9,1... | collective-permute-start | bytes 3538952 | tf_op jit(solution)/shard_map/ppermute | solution.py:309
  8.6 0.6 collective-permute-start.1
  9.2 0.3 fusion.7
  10.9 1.1 fusion.23
  12.0 0.8 fusion.39
  12.9 11.6 %collective-permute-done.1 = bf16[512,1152]{1,0:T(8,128)(2,1)S(1)} collective-permute-done((bf16[512,1152]{1,0:T(8,128)(2,1)S(1)}, bf16[512,1152]{1,0:T(8,128)(2,1)S(1)}, u32[]{:S(2)}, u32[]{:S(2)}) %collective-permute-start.1) | collective-permute-done | bytes 1179680 | tf_op jit(solution)/shard_map/ppermute | solution.py:309
  24.5 1.2 %fusion.31 = bf16[512,512]{1,0:T(8,128)(2,1)S(1)} fusion(bf16[512,1152]{1,0:T(8,128)(2,1)S(1)} %collective-permute-done.1, s32[512]{0:T(512)S(1)} %iota_add_fusion, f32[]{:T(128)} %bitcast.19, f32[]{:T(128)} %bitcast, bf16[512,1152]{1,0:T(8,128)(2,1)S(1)} %copy-done.3, f32[512]{0:T(512)S(1)} %add_rsqrt_fusion.1), kind=kOutput, calls=%fused_computation.52 | convolution fusion | flops 608894976 | bytes 2887688 | tf_op jit(solution)/shard_map/dot_general | solution.py:320
  25.7 0.9 convolution_convert_fusion.1
  26.8 1.2 %fusion.27 = bf16[512,512]{1,0:T(8,128)(2,1)S(1)} fusion(bf16[512,1152]{1,0:T(8,128)(2,1)S(1)} %collective-permute-done, s32[512]{0:T(512)S(1)} %iota_add_fusion, f32[]{:T(128)} %bitcast.20, f32[]{:T(128)} %bitcast, bf16[512,1152]{1,0:T(8,128)(2,1)S(1)} %copy-done.3, f32[512]{0:T(512)S(1)} %add_rsqrt_fusion.1), kind=kOutput, calls=%fused_computation.48 | convolution fusion | flops 608894976 | bytes 2887688 | tf_op jit(solution)/shard_map/dot_general | solution.py:320
  28.0 0.9 convolution_convert_fusion.2
  28.9 6.9 %collective-permute-start.2 = (bf16[512,1152]{1,0:T(8,128)(2,1)S(1)}, bf16[512,1152]{1,0:T(8,128)(2,1)S(1)}, u32[]{:S(2)}, u32[]{:S(2)}) collective-permute-start(bf16[512,1152]{1,0:T(8,128)(2,1)S(1)} %convolution_convert_fusion.2), channel_id=1, source_target_pairs={{1,0},{2,1},{3,2},{4,3},{5,4},{6,5},{7,6},{8,7},{9,8},{10,9},{11,1... | collective-permute-start | bytes 3538952 | tf_op jit(solution)/shard_map/ppermute | solution.py:309
  35.9 0.9 convolution_add_fusion.1
  36.7 1.1 fusion.3
  37.8 1.5 %fusion.6 = bf16[512,1152]{1,0:T(8,128)(2,1)} fusion(f32[512,1152]{1,0:T(8,128)S(1)} %get-tuple-element.6, bf16[512,1152]{1,0:T(8,128)(2,1)S(1)} %copy-done.3, f32[512]{0:T(512)S(1)} %get-tuple-element.5, f32[512]{0:T(512)S(1)} %add_rsqrt_fusion.1), kind=kLoop, calls=%fused_computation.13 | loop fusion | flops 3538944 | bytes 4722688 | tf_op jit(solution)/shard_map/convert_element_type | solution.py:384
  39.3 0.6 collective-permute-done.3
  39.9 5.2 %collective-permute-done.2 = bf16[512,1152]{1,0:T(8,128)(2,1)S(1)} collective-permute-done((bf16[512,1152]{1,0:T(8,128)(2,1)S(1)}, bf16[512,1152]{1,0:T(8,128)(2,1)S(1)}, u32[]{:S(2)}, u32[]{:S(2)}) %collective-permute-start.2) | collective-permute-done | bytes 1179680 | tf_op jit(solution)/shard_map/ppermute | solution.py:309
  45.1 1.4 %multiply_reduce_fusion = (f32[512]{0:T(512)S(1)}, f32[512,1152]{1,0:T(8,128)S(1)}) fusion(f32[512,1152]{1,0:T(8,128)S(1)} %get-tuple-element.4, f32[512]{0:T(512)S(1)} %add_rsqrt_fusion, bf16[512,1152]{1,0:T(8,128)(2,1)S(1)} %collective-permute-done.3, bf16[512,1152]{1,0:T(8,128)(2,1)S(1)} %collective-permute-done.2, bf16[512,512]{1,0:T(8,128)(2,1)S(1)} %fusion.23, ...), kind=kOutput, calls=%fused_computation.16 | convolution fusion | flops 609877504 | bytes 8787968 | tf_op jit(solution)/shard_map/dot_general | solution.py:334
  46.5 0.7 multiply_convert_fusion.hid_ref
  47.3 2.9 %convolution_convert_fusion = bf16[512,1152]{1,0:T(8,128)(2,1)} fusion(bf16[512,1152]{1,0:T(8,128)(2,1)S(1)} %multiply_convert_fusion.hid_ref, bf16[1152,1152]{1,0:T(8,128)(2,1)S(1)} %copy-done), kind=kOutput, calls=%fused_computation.2 | convolution fusion | flops 1359544320 | bytes 5013504 | tf_op jit(solution)/shard_map/dot_general | solution.py:380
  50.1 61.6 %head.1.tiles_ref = bf16[2,328,16,128]{3,2,1,0:T(8,128)(2,1)S(1)} custom-call(bf16[512,1152]{1,0:T(8,128)(2,1)S(1)} %copy-done.2, bf16[512,1152]{1,0:T(8,128)(2,1)S(1)} %multiply_convert_fusion.hid_ref), custom_call_target="tpu_custom_call" | custom-call | tf_op jit(solution)/shard_map/head/pallas_call | solution.py:274
  111.8 1.5 %copy-done.1 = bf16[2,328,16,128]{3,2,1,0:T(8,128)(2,1)} copy-done((bf16[2,328,16,128]{3,2,1,0:T(8,128)(2,1)}, bf16[2,328,16,128]{3,2,1,0:T(8,128)(2,1)S(1)}, u32[]{:S(2)}) %copy-start.1) | copy-done | bytes 2687000
  113.3 8.3 %lay_out.1 = f32[1152,1152]{1,0:T(8,128)} custom-call(bf16[2,328,16,128]{3,2,1,0:T(8,128)(2,1)} %copy-done.1), custom_call_target="tpu_custom_call" | custom-call | tf_op jit(solution)/shard_map/lay_out/pallas_call | solution.py:296
  (12 shorter events, 0.3 us)
Async XLA Ops:
  0.6 1.8 %copy-start = (bf16[1152,1152]{1,0:T(8,128)(2,1)S(1)}, bf16[1152,1152]{1,0:T(8,128)(2,1)}, u32[]{:S(2)}) copy-start(bf16[1152,1152]{1,0:T(8,128)(2,1)} %param.7) | copy-start | bytes 7962628
  5.6 3.6 %copy-start.3 = (bf16[512,1152]{1,0:T(8,128)(2,1)S(1)}, bf16[512,1152]{1,0:T(8,128)(2,1)}, u32[]{:S(2)}) copy-start(bf16[512,1152]{1,0:T(8,128)(2,1)} %param.5) | copy-start | bytes 3538948
  5.8 21.0 %collective-permute-start = (bf16[512,1152]{1,0:T(8,128)(2,1)S(1)}, bf16[512,1152]{1,0:T(8,128)(2,1)S(1)}, u32[]{:S(2)}, u32[]{:S(2)}) collective-permute-start(bf16[512,1152]{1,0:T(8,128)(2,1)S(1)} %multiply_convert_fusion.1), channel_id=1, source_target_pairs={{255,0},{0,1},{1,2},{2,3},{3,4},{4,5},{5,6},{6,7},{7,8},{8,9},{9,1... | collective-permute-start | bytes 3538952 | tf_op jit(solution)/shard_map/ppermute | solution.py:309
  8.6 15.9 %collective-permute-start.1 = (bf16[512,1152]{1,0:T(8,128)(2,1)S(1)}, bf16[512,1152]{1,0:T(8,128)(2,1)S(1)}, u32[]{:S(2)}, u32[]{:S(2)}) collective-permute-start(bf16[512,1152]{1,0:T(8,128)(2,1)S(1)} %multiply_convert_fusion.1), channel_id=1, source_target_pairs={{1,0},{2,1},{3,2},{4,3},{5,4},{6,5},{7,6},{8,7},{9,8},{10,9},{11,1... | collective-permute-start | bytes 3538952 | tf_op jit(solution)/shard_map/ppermute | solution.py:309
  26.7 13.2 %collective-permute-start.3 = (bf16[512,1152]{1,0:T(8,128)(2,1)S(1)}, bf16[512,1152]{1,0:T(8,128)(2,1)S(1)}, u32[]{:S(2)}, u32[]{:S(2)}) collective-permute-start(bf16[512,1152]{1,0:T(8,128)(2,1)S(1)} %convolution_convert_fusion.1), channel_id=1, source_target_pairs={{255,0},{0,1},{1,2},{2,3},{3,4},{4,5},{5,6},{6,7},{7,8},{8,9},{9,1... | collective-permute-start | bytes 3538952 | tf_op jit(solution)/shard_map/ppermute | solution.py:309
  28.9 16.2 %collective-permute-start.2 = (bf16[512,1152]{1,0:T(8,128)(2,1)S(1)}, bf16[512,1152]{1,0:T(8,128)(2,1)S(1)}, u32[]{:S(2)}, u32[]{:S(2)}) collective-permute-start(bf16[512,1152]{1,0:T(8,128)(2,1)S(1)} %convolution_convert_fusion.2), channel_id=1, source_target_pairs={{1,0},{2,1},{3,2},{4,3},{5,4},{6,5},{7,6},{8,7},{9,8},{10,9},{11,1... | collective-permute-start | bytes 3538952 | tf_op jit(solution)/shard_map/ppermute | solution.py:309
  47.3 2.9 %copy-start.2 = (bf16[512,1152]{1,0:T(8,128)(2,1)S(1)}, bf16[512,1152]{1,0:T(8,128)(2,1)}, u32[]{:S(2)}) copy-start(bf16[512,1152]{1,0:T(8,128)(2,1)} %txt_ref.1) | copy-start | bytes 3538948
  111.8 1.5 %copy-start.1 = (bf16[2,328,16,128]{3,2,1,0:T(8,128)(2,1)}, bf16[2,328,16,128]{3,2,1,0:T(8,128)(2,1)S(1)}, u32[]{:S(2)}) copy-start(bf16[2,328,16,128]{3,2,1,0:T(8,128)(2,1)S(1)} %head.1.tiles_ref) | copy-start | bytes 8060932

commit v2 on v1

v2 whole, which is shorter than its diff:
```python
import functools

import jax
import jax.numpy as jnp
from jax import lax
from jax.experimental import pallas as pl
from jax.experimental.pallas import tpu as pltpu
from jax.sharding import PartitionSpec as P

MESH = pl.DeviceIdType.MESH
F32 = jnp.float32
BF16 = jnp.bfloat16
ZS, XS, YS, CS = 8, 4, 4, 2
XY = XS * YS
E = 1152
ROWS = 512
HALF = E // 2
COLS = E // 128
UNITS = HALF // 16
PA = 14
PB = 13
NA = PA * XY
NB = PB * ZS
NT = NA + NB


def coords(me):
    return (me // (XS * YS * CS), (me // (YS * CS)) % XS, (me // CS) % YS, me % CS)


def device(z, x, y, c):
    return ((z * XS + x) * YS + y) * CS + c


def xy_member(me, d):
    z, x, y, c = coords(me)
    x = (x + d // YS) % XS
    y = (y + d % YS) % YS
    return (device(z, x, y, c), x * YS + y)


def xy_source(me, d):
    z, x, y, c = coords(me)
    return ((x + XS - d // YS) % XS) * YS + (y + YS - d % YS) % YS


def z_member(me, d):
    z, x, y, c = coords(me)
    z = (z + d) % ZS
    return (device(z, x, y, c), z)


def other_core(me):
    return me + 1 - 2 * (me % CS)


def remote(src, dst, ssem, rsem, to):
    return pltpu.make_async_remote_copy(
        src_ref=src, dst_ref=dst, send_sem=ssem, recv_sem=rsem,
        device_id=(to,), device_id_type=MESH,
    )


def each(lo, hi, body):
    def step(i, carry):
        body(i)
        return carry

    lax.fori_loop(lo, hi, step, 0)


def all_reduce(me, w, out, s, after_first, after_second, after_last):
    z, x, y, c = coords(me)
    p = x * YS + y
    nbr = other_core(me)

    def a1(d):
        to, q = xy_member(me, d)
        return remote(w.at[pl.ds(q * PA, PA)], s.ra1.at[d], s.s1.at[d], s.r1.at[d], to)

    def b1(d):
        to, q = z_member(me, d)
        return remote(w.at[pl.ds(NA + q * PB, PB)], s.rb1.at[d], s.s1.at[XY + d], s.r1.at[XY + d], to)

    def a2(d):
        to, q = z_member(me, d)
        return remote(s.sa.at[pl.ds(q * 2, 2)], s.ra2.at[d], s.s2.at[XY + d], s.r2.at[XY + d], to)

    def b2(d):
        to, q = xy_member(me, d)
        return remote(s.sb.at[pl.ds(q, 1)], s.rb2.at[d], s.s2.at[d], s.r2.at[d], to)

    def a3(d):
        to, q = z_member(me, d)
        here = s.ga.at[pl.ds(z * 2, 2)]
        return remote(here, here, s.s3.at[XY + d], s.r3.at[XY + d], to)

    def b3(d):
        to, q = xy_member(me, d)
        here = s.gb.at[pl.ds(p, 1)]
        return remote(here, here, s.s3.at[d], s.r3.at[d], to)

    def a4(d):
        to, q = xy_member(me, d)
        return remote(s.ga.at[pl.ds(0, PA)], out.at[c, pl.ds(p * PA, PA)], s.s4.at[d], s.r4.at[d], to)

    def b4(d):
        to, q = z_member(me, d)
        return remote(s.gb.at[pl.ds(0, PB)], out.at[c, pl.ds(NA + z * PB, PB)], s.s4.at[XY + d], s.r4.at[XY + d], to)

    def fa(d):
        q = xy_source(me, d)
        here = out.at[c, pl.ds(q * PA, PA)]
        return remote(here, here, s.s5.at[d], s.r5.at[d], nbr)

    def fb(d):
        q = z_member(me, ZS - d)[1]
        here = out.at[c, pl.ds(NA + q * PB, PB)]
        return remote(here, here, s.s5.at[XY + d], s.r5.at[XY + d], nbr)

    each(1, ZS, lambda d: b1(d).start())
    each(1, XY, lambda d: a1(d).start())
    after_first()
    each(1, ZS, lambda d: b1(d).wait_recv())

    def sum_b1(i):
        total = w[NA + z * PB + i].astype(F32) + jnp.sum(s.rb1[1:, i].astype(F32), axis=0)
        s.sb[i] = total.astype(BF16)

    each(0, PB, sum_b1)
    s.sb[PB:] = jnp.zeros((XY - PB, 16, 128), BF16)
    each(1, XY, lambda d: b2(d).start())
    each(1, XY, lambda d: a1(d).wait_recv())

    def sum_a1(i):
        total = w[p * PA + i].astype(F32) + jnp.sum(s.ra1[1:, i].astype(F32), axis=0)
        s.sa[i] = total.astype(BF16)

    each(0, PA, sum_a1)
    s.sa[PA:] = jnp.zeros((2 * ZS - PA, 16, 128), BF16)
    each(1, ZS, lambda d: a2(d).start())
    after_second()
    each(1, XY, lambda d: b2(d).wait_recv())
    total = s.sb[p].astype(F32) + jnp.sum(s.rb2[1:, 0].astype(F32), axis=0)
    s.gb[p] = total.astype(BF16)
    each(1, XY, lambda d: b3(d).start())
    each(1, ZS, lambda d: a2(d).wait_recv())

    def sum_a2(i):
        total = s.sa[z * 2 + i].astype(F32) + jnp.sum(s.ra2[1:, i].astype(F32), axis=0)
        s.ga[z * 2 + i] = total.astype(BF16)

    each(0, 2, sum_a2)
    each(1, ZS, lambda d: a3(d).start())
    each(1, XY, lambda d: b3(d).wait_recv())
    each(1, ZS, lambda d: b4(d).start())
    own_b = pltpu.make_async_copy(s.gb.at[pl.ds(0, PB)], out.at[c, pl.ds(NA + z * PB, PB)], s.own.at[0])
    own_b.start()
    each(1, ZS, lambda d: a3(d).wait_recv())
    each(1, XY, lambda d: a4(d).start())
    own_a = pltpu.make_async_copy(s.ga.at[pl.ds(0, PA)], out.at[c, pl.ds(p * PA, PA)], s.own.at[1])
    own_a.start()
    own_b.wait()
    own_a.wait()
    fb(0).start()
    fa(0).start()
    after_last()

    def pass_b(d):
        b4(d).wait_recv()
        fb(d).start()

    def pass_a(d):
        a4(d).wait_recv()
        fa(d).start()

    each(1, ZS, pass_b)
    each(1, XY, pass_a)
    for first, last in ((a1, b1), (b2, a2), (b3, a3), (a4, b4)):
        each(1, XY, lambda d: first(d).wait_send())
        each(1, ZS, lambda d: last(d).wait_send())
    each(0, XY, lambda d: fa(d).wait())
    each(0, ZS, lambda d: fb(d).wait())


class Names:
    pass


AR_SCRATCH = dict(
    ra1=pltpu.VMEM((XY, PA, 16, 128), BF16),
    rb1=pltpu.VMEM((ZS, PB, 16, 128), BF16),
    sa=pltpu.VMEM((2 * ZS, 16, 128), BF16),
    sb=pltpu.VMEM((XY, 16, 128), BF16),
    ra2=pltpu.VMEM((ZS, 2, 16, 128), BF16),
    rb2=pltpu.VMEM((XY, 1, 16, 128), BF16),
    ga=pltpu.VMEM((2 * ZS, 16, 128), BF16),
    gb=pltpu.VMEM((XY, 16, 128), BF16),
    s1=pltpu.SemaphoreType.DMA((XY + ZS,)),
    r1=pltpu.SemaphoreType.DMA((XY + ZS,)),
    s2=pltpu.SemaphoreType.DMA((XY + ZS,)),
    r2=pltpu.SemaphoreType.DMA((XY + ZS,)),
    s3=pltpu.SemaphoreType.DMA((XY + ZS,)),
    r3=pltpu.SemaphoreType.DMA((XY + ZS,)),
    s4=pltpu.SemaphoreType.DMA((XY + ZS,)),
    r4=pltpu.SemaphoreType.DMA((XY + ZS,)),
    s5=pltpu.SemaphoreType.DMA((XY + ZS,)),
    r5=pltpu.SemaphoreType.DMA((XY + ZS,)),
    own=pltpu.SemaphoreType.DMA((2,)),
)


def greet_all(me):
    barrier = pltpu.get_barrier_semaphore()

    def greet(to):
        pl.semaphore_signal(barrier, inc=1, device_id=(to,), device_id_type=MESH)

    greet(far_device(me))
    greet(other_core(me))
    each(1, XY, lambda d: greet(xy_member(me, d)[0]))
    each(1, ZS, lambda d: greet(z_member(me, d)[0]))
    return barrier


RC = 128
FAR = 256


def far_device(me):
    ring = ZS * XS * YS * CS
    return lax.rem(me + ring - 1 + 2 * (me % CS), ring)


def rows_at(start, size):
    return pl.ds(pl.multiple_of(start, size), size)


def dot_nt(a, b):
    return lax.dot_general(a, b, (((1,), (1,)), ((), ())), preferred_element_type=F32)


def dot_nn(a, b):
    return jnp.dot(a, b, preferred_element_type=F32)


def unit_of(values):
    rinv = lax.rsqrt(jnp.sum(values * values, axis=-1, keepdims=True) + 1e-06)
    return (values * rinv, rinv)


def own_diagonal(shape, start):
    row = lax.broadcasted_iota(jnp.int32, shape, 0) + start
    return lax.broadcasted_iota(jnp.int32, shape, 1) == row


def main_kernel(img_hbm, feat_hbm, head_hbm, scale_ref, bias_ref, tiles, txt_out, img_out, *scratch):
    me = lax.axis_index("batch")
    c = me % CS
    near = other_core(me)
    far = far_device(me)
    s = Names()
    for name, ref in zip(list(MAIN_SCRATCH), scratch):
        setattr(s, name, ref)
    img_in = pltpu.make_async_copy(img_hbm, s.img, s.ins.at[0])
    feat_in = pltpu.make_async_copy(feat_hbm, s.feat, s.ins.at[1])
    head_in = pltpu.make_async_copy(head_hbm, s.head, s.ins.at[2])
    img_in.start()
    feat_in.start()
    head_in.start()
    barrier = greet_all(me)
    half = 0.5 * jnp.exp(jnp.full((1, 1), scale_ref[0], F32))
    shift = 0.5 * jnp.full((1, 1), bias_ref[0], F32)

    def weights(dots):
        return jnp.tanh(dots * half + shift) * half + half

    def img_far(k):
        return remote(s.imgs.at[pl.ds(k * FAR, FAR)], s.imgs.at[pl.ds(2 * ROWS + k * FAR, FAR)],
                      s.es.at[k], s.er.at[k], far)

    def txt_far(k):
        return remote(s.txts.at[pl.ds(k * FAR, FAR)], s.txts.at[pl.ds(2 * ROWS + k * FAR, FAR)],
                      s.es.at[2 + k], s.er.at[2 + k], far)

    img_near = remote(s.imgs.at[pl.ds(0, ROWS)], s.imgs.at[pl.ds(ROWS, ROWS)], s.es.at[4], s.er.at[4], near)
    txt_near = remote(s.txts.at[pl.ds(0, ROWS)], s.txts.at[pl.ds(ROWS, ROWS)], s.es.at[5], s.er.at[5], near)
    theirs = rows_at((1 - c) * HALF, HALF)
    feat_near = remote(s.feat_t.at[theirs], s.feat_nbr, s.es.at[6], s.er.at[6], near)

    def hid_near(j):
        return remote(s.hid.at[rows_at(j * RC, RC)], s.hid.at[rows_at(ROWS + j * RC, RC)],
                      s.hs.at[j], s.hr.at[j], near)

    img_in.wait()

    def unit_images(j):
        at = rows_at(j * RC, RC)
        unit, rinv = unit_of(s.img[at, :].astype(F32))
        s.imgs[at, :] = unit.astype(BF16)
        s.img_rinv[at, :] = rinv

    each(0, FAR // RC, unit_images)
    pl.semaphore_wait(barrier, XY + ZS)
    img_far(0).start()
    each(FAR // RC, ROWS // RC, unit_images)
    img_far(1).start()
    img_near.start()
    feat_in.wait()
    head_in.wait()

    def unit_texts(j):
        at = rows_at(j * RC, RC)
        unit, rinv = unit_of(dot_nn(s.feat[at, :], s.head[...]))
        s.txt_unit[at, :] = unit
        s.txts[at, :] = unit.astype(BF16)
        s.txt_rinv[at, :] = rinv

    each(0, ROWS // RC, unit_texts)
    txt_near.start()

    def flip(i):
        cols = rows_at(i * 128, 128)
        s.feat_t[cols, :] = s.feat[:, cols].T

    each(0, COLS, flip)
    feat_near.start()
    img_near.wait_recv()

    def text_first(j):
        at = rows_at(j * RC, RC)
        images = s.imgs[0:2 * ROWS, :]
        weight = weights(dot_nt(s.txts[at, :], images))
        weight = weight - jnp.where(own_diagonal(weight.shape, j * RC), 2.0 * half, 0.0)
        s.text_sum[at, :] = dot_nn(weight.astype(BF16), images)

    each(0, ROWS // RC, text_first)
    img_far(0).wait_recv()

    def text_second(j):
        at = rows_at(j * RC, RC)
        images = s.imgs[2 * ROWS:2 * ROWS + FAR, :]
        weight = weights(dot_nt(s.txts[at, :], images)).astype(BF16)
        s.text_sum[at, :] += dot_nn(weight, images)

    each(0, ROWS // RC, text_second)
    img_far(1).wait_recv()

    def text_third(j):
        at = rows_at(j * RC, RC)
        images = s.imgs[2 * ROWS + FAR:3 * ROWS, :]
        weight = weights(dot_nt(s.txts[at, :], images)).astype(BF16)
        total = s.text_sum[at, :] + dot_nn(weight, images)
        unit = s.txt_unit[at, :]
        along = jnp.sum(unit * total, axis=-1, keepdims=True)
        s.hid[at, :] = ((total - unit * along) * s.txt_rinv[at, :]).astype(BF16)
        hid_near(j).start()

    each(0, ROWS // RC, text_third)
    step = 6
    block = 16 * step

    def head_own(i):
        mine = s.feat_t[rows_at(c * HALF + i * block, block), :]
        s.head_sum[rows_at(i * block, block), :] = dot_nn(mine, s.hid[0:ROWS, :])

    each(0, UNITS // step, head_own)
    feat_near.wait_recv()
    each(0, ROWS // RC, lambda j: hid_near(j).wait_recv())

    def head_near(i):
        at = rows_at(i * block, block)
        value = s.head_sum[at, :] + dot_nn(s.feat_nbr[at, :], s.hid[ROWS:2 * ROWS, :])
        value = value.astype(BF16)
        for r in range(step):
            for col in range(COLS):
                s.w[(i * step + r) * COLS + col] = value[r * 16:(r + 1) * 16, col * 128:(col + 1) * 128]

    each(0, UNITS // step, head_near)
    s.w[UNITS * COLS:] = jnp.zeros((NT - UNITS * COLS, 16, 128), BF16)

    txt_write = pltpu.make_async_copy(s.txt_grad, txt_out, s.outs.at[0])
    img_write = pltpu.make_async_copy(s.img_grad, img_out, s.outs.at[1])

    def after_first():
        def text_grads(j):
            at = rows_at(j * RC, RC)
            s.txt_grad[at, :] = dot_nt(s.hid[at, :], s.head[...]).astype(BF16)

        each(0, ROWS // RC, text_grads)
        txt_write.start()
        txt_near.wait_recv()

        def image_first(j):
            at = rows_at(j * RC, RC)
            texts = s.txts[0:2 * ROWS, :]
            weight = weights(dot_nt(s.imgs[at, :], texts))
            weight = weight - jnp.where(own_diagonal(weight.shape, j * RC), 2.0 * half, 0.0)
            s.img_sum[at, :] = dot_nn(weight.astype(BF16), texts)

        each(0, ROWS // RC, image_first)

    def after_second():
        txt_far(0).start()
        txt_far(1).start()

    def after_last():
        txt_far(0).wait_recv()
        txt_far(1).wait_recv()

        def image_second(j):
            at = rows_at(j * RC, RC)
            texts = s.txts[2 * ROWS:3 * ROWS, :]
            weight = weights(dot_nt(s.imgs[at, :], texts)).astype(BF16)
            total = s.img_sum[at, :] + dot_nn(weight, texts)
            rinv = s.img_rinv[at, :]
            unit = s.img[at, :].astype(F32) * rinv
            along = jnp.sum(unit * total, axis=-1, keepdims=True)
            s.img_grad[at, :] = ((total - unit * along) * rinv).astype(BF16)

        each(0, ROWS // RC, image_second)
        img_write.start()

    all_reduce(me, s.w, tiles, s, after_first, after_second, after_last)
    for k in range(2):
        img_far(k).wait_send()
        txt_far(k).wait_send()
    img_near.wait_send()
    txt_near.wait_send()
    feat_near.wait_send()
    each(0, ROWS // RC, lambda j: hid_near(j).wait_send())
    txt_write.wait()
    img_write.wait()


MAIN_SCRATCH = dict(
    img=pltpu.VMEM((ROWS, E), BF16),
    feat=pltpu.VMEM((ROWS, E), BF16),
    head=pltpu.VMEM((E, E), BF16),
    imgs=pltpu.VMEM((3 * ROWS, E), BF16),
    txts=pltpu.VMEM((3 * ROWS, E), BF16),
    img_rinv=pltpu.VMEM((ROWS, 1), F32),
    txt_rinv=pltpu.VMEM((ROWS, 1), F32),
    txt_unit=pltpu.VMEM((ROWS, E), F32),
    text_sum=pltpu.VMEM((ROWS, E), F32),
    img_sum=pltpu.VMEM((ROWS, E), F32),
    hid=pltpu.VMEM((2 * ROWS, E), BF16),
    feat_t=pltpu.VMEM((E, ROWS), BF16),
    feat_nbr=pltpu.VMEM((HALF, ROWS), BF16),
    head_sum=pltpu.VMEM((HALF, E), F32),
    w=pltpu.VMEM((NT, 16, 128), BF16),
    txt_grad=pltpu.VMEM((ROWS, E), BF16),
    img_grad=pltpu.VMEM((ROWS, E), BF16),
    ins=pltpu.SemaphoreType.DMA((3,)),
    outs=pltpu.SemaphoreType.DMA((2,)),
    es=pltpu.SemaphoreType.DMA((7,)),
    er=pltpu.SemaphoreType.DMA((7,)),
    hs=pltpu.SemaphoreType.DMA((4,)),
    hr=pltpu.SemaphoreType.DMA((4,)),
    **AR_SCRATCH,
)


def main_call(img_emb, txt_feat, txt_head, log_scale, bias):
    return pl.pallas_call(
        main_kernel,
        out_shape=(
            jax.ShapeDtypeStruct((CS, NT, 16, 128), BF16),
            jax.ShapeDtypeStruct((ROWS, E), BF16),
            jax.ShapeDtypeStruct((ROWS, E), BF16),
        ),
        in_specs=[pl.BlockSpec(memory_space=pl.ANY)] * 3 + [pl.BlockSpec(memory_space=pltpu.SMEM)] * 2,
        out_specs=[pl.BlockSpec(memory_space=pl.ANY)] * 3,
        scratch_shapes=list(MAIN_SCRATCH.values()),
        compiler_params=pltpu.CompilerParams(
            collective_id=0, has_side_effects=True, vmem_limit_bytes=56 << 20
        ),
        name="main",
    )(img_emb, txt_feat, txt_head, log_scale, bias)


LAY = 96


def final_kernel(tiles_hbm, txt_hbm, img_hbm, head_out, txt_out, img_out, tiles, head, txt, img, sems):
    txt_in = pltpu.make_async_copy(txt_hbm, txt, sems.at[0])
    img_in = pltpu.make_async_copy(img_hbm, img, sems.at[1])
    txt_back = pltpu.make_async_copy(txt, txt_out, sems.at[2])
    img_back = pltpu.make_async_copy(img, img_out, sems.at[3])
    per = LAY // 16 * COLS
    blocks = HALF // LAY

    def read(i):
        at = pl.ds((i % blocks) * per, per)
        return pltpu.make_async_copy(tiles_hbm.at[i // blocks, at], tiles.at[i // blocks, at], sems.at[4 + i])

    def write(i):
        at = rows_at(i * LAY, LAY)
        return pltpu.make_async_copy(head.at[at], head_out.at[at], sems.at[4 + CS * blocks + i])

    each(0, CS * blocks, lambda i: read(i).start())
    txt_in.start()
    img_in.start()

    def lay(i):
        read(i).wait()
        for r in range(LAY // 16):
            for col in range(COLS):
                value = tiles[i // blocks, (i % blocks) * per + r * COLS + col]
                head[pl.ds(pl.multiple_of(i * LAY + r * 16, 16), 16), col * 128:(col + 1) * 128] = value.astype(F32)
        write(i).start()

    each(0, CS * blocks, lay)
    txt_in.wait()
    txt_back.start()
    img_in.wait()
    img_back.start()
    each(0, CS * blocks, lambda i: write(i).wait())
    txt_back.wait()
    img_back.wait()


def final_call(tiles, txt_grad, img_grad):
    return pl.pallas_call(
        final_kernel,
        out_shape=(
            jax.ShapeDtypeStruct((E, E), F32),
            jax.ShapeDtypeStruct((ROWS, E), BF16),
            jax.ShapeDtypeStruct((ROWS, E), BF16),
        ),
        in_specs=[pl.BlockSpec(memory_space=pl.ANY)] * 3,
        out_specs=[pl.BlockSpec(memory_space=pl.ANY)] * 3,
        scratch_shapes=[
            pltpu.VMEM((CS, NT, 16, 128), BF16),
            pltpu.VMEM((E, E), F32),
            pltpu.VMEM((ROWS, E), BF16),
            pltpu.VMEM((ROWS, E), BF16),
            pltpu.SemaphoreType.DMA((4 + 2 * CS * HALF // LAY,)),
        ],
        compiler_params=pltpu.CompilerParams(vmem_limit_bytes=56 << 20),
        name="final",
    )(tiles, txt_grad, img_grad)


def shards(img_emb, txt_feat, txt_head, log_scale, bias):
    tiles, txt_grad, img_grad = main_call(img_emb, txt_feat, txt_head, log_scale, bias)
    head_grad, txt_grad, img_grad = final_call(tiles, txt_grad, img_grad)
    return (img_grad, txt_grad, head_grad)


def solution(mesh):
    return jax.shard_map(
        shards,
        mesh=mesh,
        in_specs=(P("batch", None), P("batch", None), P(), P(), P()),
        out_specs=(P("batch", None), P("batch", None), P()),
        check_vma=False,
    )
```

time: 122 us -> 91.8 us (0.75)
  Pallas kernels: 69.9 us -> 89.7 us
  waiting for transfers between devices: 17.4 us -> 0 us
  matrix products: 15.7 us -> 0 us
  starting transfers between devices: 10.4 us -> 0 us
  local copies, waits for them, and re-layouts: 3.28 us -> 0 us
  other arithmetic: 2.76 us -> 0 us
    pallas_call x2, Pallas kernels: 69.9 us -> 89.7 us  [the longest x1 84.2 us: main_call(): pl.pallas_call(main_kernel, out_shape=(jax.ShapeDtypeStruct((CS, NT, 16,...]
    ppermute x4 -> x0, waiting for transfers between devices: 17.4 us -> none  [passed_along(): return lax.ppermute(block, axis, route)]
    dot_general x11 -> x0, matrix products: 15.7 us -> none  [the longest x3 3.58 us: pair_weights(): lax.dot_general(images, texts, (((1,), (1,)), ((), ())), preferred_elemen...]
    ppermute x4 -> x0, starting transfers between devices: 10.4 us -> none  [passed_along(): return lax.ppermute(block, axis, route)]
    unnamed x8 -> x0, local copies, waits for them, and re-layouts: 3.28 us -> none
    convert_element_type x3 -> x0, other arithmetic: 2.45 us -> none  [the longest x1 1.51 us: shards(): img_grad.astype(jnp.bfloat16)]
  transfers between devices with their start and end apart: 4 -> 0, of which waited for: 3 -> 0; matrix products, arithmetic and copies ran while one was open for 8% -> 0% of each run, Pallas kernels for 0% -> 0%
where the time goes in v2:
time: 91.8 us; the launch traced here: 91.6 us
  Pallas kernels  89.7 us (98%)
  between operations  1.93 us (2%)
    pallas_call x1, Pallas kernels, main_call(): pl.pallas_call(main_kernel, out_shape=(jax.ShapeDtypeStruct((CS, NT, 16,...  84.2 us
    pallas_call x1, Pallas kernels, final_call(): pl.pallas_call(final_kernel, out_shape=(jax.ShapeDtypeStruct((E, E), F32)...  5.46 us

profile of v2, /device:TPU:1, one launch (start us, length us, event | category | flops | bytes accessed | tf_op | source)
XLA Modules:
  0.0 91.6 jit_solution(3452518301384590729)
XLA Ops:
  1.9 84.2 %main.1 = (bf16[2,328,16,128]{3,2,1,0:T(8,128)(2,1)}, bf16[512,1152]{1,0:T(8,128)(2,1)}, bf16[512,1152]{1,0:T(8,128)(2,1)}) custom-call(bf16[512,1152]{1,0:T(8,128)(2,1)} %img_hbm.1, bf16[512,1152]{1,0:T(8,128)(2,1)} %feat_hbm.1, bf16[1152,1152]{1,0:T(8,128)(2,1)} %head_hbm.1, f32[1]{0:T(128)S(6)} %copy.8.scale_ref, f32[1]{0:T(128)S(6)} %copy.9.bias_ref), custom_call_target="tpu_custom_call" | custom-call | tf_op jit(solution)/shard_map/main/pallas_call | solution.py:465
  86.2 5.5 %final.1 = (f32[1152,1152]{1,0:T(8,128)}, bf16[512,1152]{1,0:T(8,128)(2,1)}, bf16[512,1152]{1,0:T(8,128)(2,1)}) custom-call(bf16[2,328,16,128]{3,2,1,0:T(8,128)(2,1)} %get-tuple-element.9.tiles_hbm, bf16[512,1152]{1,0:T(8,128)(2,1)} %get-tuple-element.10.txt_hbm, bf16[512,1152]{1,0:T(8,128)(2,1)} %get-tuple-element.11.img_hbm), custom_call_target="tpu_custom_call" | custom-call | tf_op jit(solution)/shard_map/final/pallas_call | solution.py:524

commit v3 on v2

v3 whole, which is shorter than its diff:
```python
import functools

import jax
import jax.numpy as jnp
from jax import lax
from jax.experimental import pallas as pl
from jax.experimental.pallas import tpu as pltpu
from jax.sharding import PartitionSpec as P

MESH = pl.DeviceIdType.MESH
F32 = jnp.float32
BF16 = jnp.bfloat16
ZS, XS, YS, CS = 8, 4, 4, 2
XY = XS * YS
E = 1152
ROWS = 512
HALF = E // 2
COLS = E // 128
UNITS = HALF // 16
NT = 328


def coords(me):
    return (me // (XS * YS * CS), (me // (YS * CS)) % XS, (me // CS) % YS, me % CS)


def device(z, x, y, c):
    return ((z * XS + x) * YS + y) * CS + c


def xy_member(me, d):
    z, x, y, c = coords(me)
    x = (x + d // YS) % XS
    y = (y + d % YS) % YS
    return (device(z, x, y, c), x * YS + y)


def xy_source(me, d):
    z, x, y, c = coords(me)
    return ((x + XS - d // YS) % XS) * YS + (y + YS - d % YS) % YS


def z_member(me, d):
    z, x, y, c = coords(me)
    z = (z + d) % ZS
    return (device(z, x, y, c), z)


def z_source(me, d):
    return (coords(me)[0] + ZS - d) % ZS


def other_core(me):
    return me + 1 - 2 * (me % CS)


def far_device(me):
    ring = ZS * XS * YS * CS
    return lax.rem(me + ring - 1 + 2 * (me % CS), ring)


def remote(src, dst, ssem, rsem, to):
    return pltpu.make_async_remote_copy(
        src_ref=src, dst_ref=dst, send_sem=ssem, recv_sem=rsem,
        device_id=(to,), device_id_type=MESH,
    )


def each(lo, hi, body):
    def step(i, carry):
        body(i)
        return carry

    lax.fori_loop(lo, hi, step, 0)


class Names:
    pass


XY_AXIS = (XY, xy_member, xy_source)
Z_AXIS = (ZS, z_member, z_source)


class Stream:
    def __init__(self, name, start, per, first, second):
        self.name = name
        self.start = start
        self.per = per
        self.first = first
        self.second = second

    def scratch(self):
        n, m = self.first[0], self.second[0]
        return {
            self.name + "_got": pltpu.VMEM((n, self.per, 16, 128), BF16),
            self.name + "_part": pltpu.VMEM((m, 16, 128), BF16),
            self.name + "_got2": pltpu.VMEM((m, 1, 16, 128), BF16),
            self.name + "_sum": pltpu.VMEM((m, 16, 128), BF16),
            self.name + "_send": pltpu.SemaphoreType.DMA((5, XY)),
            self.name + "_recv": pltpu.SemaphoreType.DMA((5, XY)),
        }

    def bind(self, me, w, out, s):
        self.me, self.w, self.out = me, w, out
        self.got, self.part, self.got2, self.sum, self.send, self.recv = (
            getattr(s, self.name + "_" + kind) for kind in ("got", "part", "got2", "sum", "send", "recv")
        )
        self.c = coords(me)[3]
        self.p = self.first[1](me, 0)[1]
        self.q = self.second[1](me, 0)[1]

    def copy(self, phase, src, dst, d, to):
        return remote(src, dst, self.send.at[phase, d], self.recv.at[phase, d], to)

    def scatter(self, d):
        to, q = self.first[1](self.me, d)
        return self.copy(0, self.w.at[pl.ds(self.start + q * self.per, self.per)], self.got.at[d], d, to)

    def scatter2(self, d):
        to, q = self.second[1](self.me, d)
        return self.copy(1, self.part.at[pl.ds(q, 1)], self.got2.at[d], d, to)

    def gather2(self, d):
        to, q = self.second[1](self.me, d)
        here = self.sum.at[pl.ds(self.q, 1)]
        return self.copy(2, here, here, d, to)

    def piece(self, q):
        return self.out.at[self.c, pl.ds(self.start + q * self.per, self.per)]

    def gather(self, d):
        to, q = self.first[1](self.me, d)
        return self.copy(3, self.sum.at[pl.ds(0, self.per)], self.piece(self.p), d, to)

    def own(self):
        return pltpu.make_async_copy(self.sum.at[pl.ds(0, self.per)], self.piece(self.p), self.send.at[3, 0])

    def hand(self, d):
        here = self.piece(self.first[2](self.me, d))
        return self.copy(4, here, here, d, other_core(self.me))

    def start_scatter(self):
        each(1, self.first[0], lambda d: self.scatter(d).start())

    def start_scatter2(self):
        each(1, self.first[0], lambda d: self.scatter(d).wait_recv())

        def add(i):
            total = self.w[self.start + self.p * self.per + i].astype(F32)
            total += jnp.sum(self.got[1:, i].astype(F32), axis=0)
            self.part[i] = total.astype(BF16)

        each(0, self.per, add)
        m = self.second[0]
        if m > self.per:
            self.part[self.per:] = jnp.zeros((m - self.per, 16, 128), BF16)
        each(1, m, lambda d: self.scatter2(d).start())

    def start_gather2(self):
        m = self.second[0]
        each(1, m, lambda d: self.scatter2(d).wait_recv())
        total = self.part[self.q].astype(F32) + jnp.sum(self.got2[1:, 0].astype(F32), axis=0)
        self.sum[self.q] = total.astype(BF16)
        each(1, m, lambda d: self.gather2(d).start())

    def start_gather(self):
        each(1, self.second[0], lambda d: self.gather2(d).wait_recv())
        each(1, self.first[0], lambda d: self.gather(d).start())
        self.own().start()

    def pass_own(self):
        self.own().wait()
        self.hand(0).start()

    def pass_on(self):
        def move(d):
            self.gather(d).wait_recv()
            self.hand(d).start()

        each(1, self.first[0], move)

    def finish(self):
        n, m = self.first[0], self.second[0]
        each(1, n, lambda d: self.scatter(d).wait_send())
        each(1, m, lambda d: self.scatter2(d).wait_send())
        each(1, m, lambda d: self.gather2(d).wait_send())
        each(1, n, lambda d: self.gather(d).wait_send())
        each(0, n, lambda d: self.hand(d).wait())


def streams():
    return (
        Stream("a1", 0, 7, XY_AXIS, Z_AXIS),
        Stream("b1", 112, 6, Z_AXIS, XY_AXIS),
        Stream("a2", 160, 7, XY_AXIS, Z_AXIS),
        Stream("b2", 272, 7, Z_AXIS, XY_AXIS),
    )


def greet_all(me):
    barrier = pltpu.get_barrier_semaphore()

    def greet(to):
        pl.semaphore_signal(barrier, inc=1, device_id=(to,), device_id_type=MESH)

    greet(far_device(me))
    greet(other_core(me))
    each(1, XY, lambda d: greet(xy_member(me, d)[0]))
    each(1, ZS, lambda d: greet(z_member(me, d)[0]))
    return barrier


RC = 128
EARLY = 256
NC = ROWS // RC
CW = 384
TAIL = 256
HB = 288


def rows_at(start, size):
    return pl.ds(pl.multiple_of(start, size), size)


def dot_nt(a, b):
    return lax.dot_general(a, b, (((1,), (1,)), ((), ())), preferred_element_type=F32)


def dot_nn(a, b):
    return jnp.dot(a, b, preferred_element_type=F32)


def unit_of(values):
    rinv = lax.rsqrt(jnp.sum(values * values, axis=-1, keepdims=True) + 1e-06)
    return (values * rinv, rinv)


def own_diagonal(shape):
    row = lax.broadcasted_iota(jnp.int32, shape, 0)
    return lax.broadcasted_iota(jnp.int32, shape, 1) == row


def across(total, unit, rinv):
    along = jnp.sum(unit * total, axis=-1, keepdims=True)
    return ((total - unit * along) * rinv).astype(BF16)


def main_kernel(img_hbm, feat_hbm, head_hbm, scale_ref, bias_ref, tiles, txt_out, img_out, *scratch):
    me = lax.axis_index("batch")
    c = me % CS
    near = other_core(me)
    far = far_device(me)
    s = Names()
    for name, ref in zip(list(MAIN_SCRATCH), scratch):
        setattr(s, name, ref)
    a1, b1, a2, b2 = lines = streams()
    for line in lines:
        line.bind(me, s.w, tiles, s)
    img_in = pltpu.make_async_copy(img_hbm, s.img, s.ins.at[0])
    feat_in = pltpu.make_async_copy(feat_hbm, s.feat, s.ins.at[1])
    head_in = pltpu.make_async_copy(head_hbm, s.head, s.ins.at[2])
    img_in.start()
    feat_in.start()
    head_in.start()
    barrier = greet_all(me)
    half = 0.5 * jnp.exp(jnp.full((1, 1), scale_ref[0], F32))
    shift = 0.5 * jnp.full((1, 1), bias_ref[0], F32)

    def weights(left, right, diagonal=False):
        weight = jnp.tanh(dot_nt(left, right) * half + shift) * half + half
        if diagonal:
            weight = weight - jnp.where(own_diagonal(weight.shape), 2.0 * half, 0.0)
        return weight.astype(BF16)

    def img_far(j):
        start, size = ((0, 2 * RC), (2 * RC, RC), (3 * RC, RC))[j]
        return remote(s.imgs.at[pl.ds(start, size)], s.imgs.at[pl.ds(2 * ROWS + start, size)],
                      s.es.at[j], s.er.at[j], far)

    def txt_far(j):
        start, size = ((0, EARLY), (EARLY, ROWS - EARLY))[j]
        return remote(s.txts.at[pl.ds(start, size)], s.txts.at[pl.ds(2 * ROWS + start, size)],
                      s.es.at[NC + j], s.er.at[NC + j], far)

    n = 2 * NC
    img_near = remote(s.imgs.at[pl.ds(0, ROWS)], s.imgs.at[pl.ds(ROWS, ROWS)], s.es.at[n], s.er.at[n], near)
    txt_near = remote(s.txts.at[pl.ds(0, ROWS)], s.txts.at[pl.ds(ROWS, ROWS)], s.es.at[n + 1], s.er.at[n + 1], near)
    theirs = rows_at((1 - c) * HALF, HALF)
    feat_near = remote(s.feat_t.at[theirs], s.feat_nbr, s.es.at[n + 2], s.er.at[n + 2], near)

    def hid_near(k):
        return remote(s.hid.at[pl.ds(k * TAIL, TAIL)], s.hid.at[pl.ds(ROWS + k * TAIL, TAIL)],
                      s.es.at[n + 3 + k], s.er.at[n + 3 + k], near)

    img_in.wait()

    def unit_images(j):
        at = pl.ds(j * RC, RC)
        unit, rinv = unit_of(s.img[at, :].astype(F32))
        s.imgs[at, :] = unit.astype(BF16)
        s.img_rinv[at, :] = rinv

    unit_images(0)
    unit_images(1)
    pl.semaphore_wait(barrier, XY + ZS)
    img_far(0).start()
    unit_images(2)
    img_far(1).start()
    unit_images(3)
    img_far(2).start()
    img_near.start()
    feat_in.wait()
    head_in.wait()
    s.txt_unit[...] = dot_nn(s.feat[...], s.head[...])

    def unit_texts(j):
        at = rows_at(j * RC, RC)
        unit, rinv = unit_of(s.txt_unit[at, :])
        s.txt_unit[at, :] = unit
        s.txts[at, :] = unit.astype(BF16)
        s.txt_rinv[at, :] = rinv

    each(0, NC, unit_texts)
    txt_near.start()
    txt_far(0).start()

    own = pl.ds(0, ROWS)
    nbr = pl.ds(ROWS, ROWS)
    s.wt[:, 0:ROWS] = weights(s.txts[own, :], s.imgs[own, :], True)

    def flip(i):
        cols = rows_at(i * 128, 128)
        s.feat_t[cols, :] = s.feat[:, cols].T

    each(0, COLS, flip)
    feat_near.start()
    img_near.wait_recv()
    s.wt[:, ROWS:2 * ROWS] = weights(s.txts[own, :], s.imgs[nbr, :])

    def sums_of(sums, block, first, size, add):
        def columns(i):
            cols = rows_at(i * CW, CW)
            value = dot_nn(s.wt[:, first:first + size], block[first:first + size, cols])
            sums[:, cols] = sums[:, cols] + value if add else value

        each(0, E // CW, columns)

    sums_of(s.text_sum, s.imgs, 0, 2 * ROWS, False)
    base = 2 * ROWS
    img_far(0).wait_recv()
    s.wt[:, base:base + 2 * RC] = weights(s.txts[own, :], s.imgs[pl.ds(base, 2 * RC), :])
    img_far(1).wait_recv()
    s.wt[:, base + 2 * RC:base + 3 * RC] = weights(s.txts[own, :], s.imgs[pl.ds(base + 2 * RC, RC), :])
    sums_of(s.text_sum, s.imgs, base, 3 * RC, True)
    img_far(2).wait_recv()
    last = pl.ds(base + 3 * RC, RC)
    for k in range(ROWS // TAIL):
        at = pl.ds(k * TAIL, TAIL)
        weight = weights(s.txts[at, :], s.imgs[last, :])
        total = s.text_sum[at, :] + dot_nn(weight, s.imgs[last, :])
        s.hid[at, :] = across(total, s.txt_unit[at, :], s.txt_rinv[at, :])
        hid_near(k).start()

    def head_own(i):
        mine = s.feat_t[rows_at(c * HALF + i * HB, HB), :]
        s.head_sum[rows_at(i * HB, HB), :] = dot_nn(mine, s.hid[own, :])

    each(0, HALF // HB, head_own)
    feat_near.wait_recv()
    for k in range(ROWS // TAIL):
        hid_near(k).wait_recv()

    def head_both(i):
        at = pl.ds(i * HB, HB)
        value = s.head_sum[at, :] + dot_nn(s.feat_nbr[at, :], s.hid[nbr, :])
        value = value.astype(BF16)
        for r in range(HB // 16):
            for col in range(COLS):
                s.w[(i * HB // 16 + r) * COLS + col] = value[r * 16:(r + 1) * 16, col * 128:(col + 1) * 128]

    head_both(0)
    b1.start_scatter()
    a1.start_scatter()
    head_both(1)
    s.w[UNITS * COLS:] = jnp.zeros((NT - UNITS * COLS, 16, 128), BF16)
    b2.start_scatter()
    a2.start_scatter()

    txt_write = pltpu.make_async_copy(s.txt_grad, txt_out, s.outs.at[0])
    img_write = pltpu.make_async_copy(s.img_grad, img_out, s.outs.at[1])

    def text_grads(i):
        cols = rows_at(i * CW, CW)
        s.txt_grad[:, cols] = dot_nt(s.hid[own, :], s.head[cols, :]).astype(BF16)

    each(0, E // CW, text_grads)
    txt_write.start()
    s.wt[:, 0:ROWS] = weights(s.imgs[own, :], s.txts[own, :], True)
    txt_near.wait_recv()
    s.wt[:, ROWS:2 * ROWS] = weights(s.imgs[own, :], s.txts[nbr, :])
    sums_of(s.img_sum, s.txts, 0, 2 * ROWS, False)

    def image_far(j):
        start, size = ((0, EARLY), (EARLY, ROWS - EARLY))[j]
        txt_far(j).wait_recv()
        s.wt[:, base + start:base + start + size] = weights(s.imgs[own, :], s.txts[pl.ds(base + start, size), :])
        sums_of(s.img_sum, s.txts, base + start, size, True)

    image_far(0)

    for line in (b1, a1, b2, a2):
        line.start_scatter2()
    txt_far(1).start()
    for line in (b1, a1, b2, a2):
        line.start_gather2()
    for line in (b1, a1, b2, a2):
        line.start_gather()
    for line in (b1, a1, b2, a2):
        line.pass_own()
    b1.pass_on()
    a1.pass_on()
    image_far(1)
    def image_grads(j):
        at = rows_at(j * RC, RC)
        rinv = s.img_rinv[at, :]
        s.img_grad[at, :] = across(s.img_sum[at, :], s.img[at, :].astype(F32) * rinv, rinv)

    each(0, NC, image_grads)
    img_write.start()
    b2.pass_on()
    a2.pass_on()
    for line in lines:
        line.finish()
    for j in range(3):
        img_far(j).wait_send()
    for j in range(2):
        txt_far(j).wait_send()
    img_near.wait_send()
    txt_near.wait_send()
    feat_near.wait_send()
    for k in range(ROWS // TAIL):
        hid_near(k).wait_send()
    txt_write.wait()
    img_write.wait()


MAIN_SCRATCH = dict(
    img=pltpu.VMEM((ROWS, E), BF16),
    feat=pltpu.VMEM((ROWS, E), BF16),
    head=pltpu.VMEM((E, E), BF16),
    imgs=pltpu.VMEM((3 * ROWS, E), BF16),
    txts=pltpu.VMEM((3 * ROWS, E), BF16),
    wt=pltpu.VMEM((ROWS, 3 * ROWS), BF16),
    img_rinv=pltpu.VMEM((ROWS, 1), F32),
    txt_rinv=pltpu.VMEM((ROWS, 1), F32),
    txt_unit=pltpu.VMEM((ROWS, E), F32),
    text_sum=pltpu.VMEM((ROWS, E), F32),
    img_sum=pltpu.VMEM((ROWS, E), F32),
    hid=pltpu.VMEM((2 * ROWS, E), BF16),
    feat_t=pltpu.VMEM((E, ROWS), BF16),
    feat_nbr=pltpu.VMEM((HALF, ROWS), BF16),
    head_sum=pltpu.VMEM((HALF, E), F32),
    w=pltpu.VMEM((NT, 16, 128), BF16),
    txt_grad=pltpu.VMEM((ROWS, E), BF16),
    img_grad=pltpu.VMEM((ROWS, E), BF16),
    ins=pltpu.SemaphoreType.DMA((3,)),
    outs=pltpu.SemaphoreType.DMA((2,)),
    es=pltpu.SemaphoreType.DMA((2 * NC + 5,)),
    er=pltpu.SemaphoreType.DMA((2 * NC + 5,)),
)
for line in streams():
    MAIN_SCRATCH.update(line.scratch())


def main_call(img_emb, txt_feat, txt_head, log_scale, bias):
    return pl.pallas_call(
        main_kernel,
        out_shape=(
            jax.ShapeDtypeStruct((CS, NT, 16, 128), BF16),
            jax.ShapeDtypeStruct((ROWS, E), BF16),
            jax.ShapeDtypeStruct((ROWS, E), BF16),
        ),
        in_specs=[pl.BlockSpec(memory_space=pl.ANY)] * 3 + [pl.BlockSpec(memory_space=pltpu.SMEM)] * 2,
        out_specs=[pl.BlockSpec(memory_space=pl.ANY)] * 3,
        scratch_shapes=list(MAIN_SCRATCH.values()),
        compiler_params=pltpu.CompilerParams(
            collective_id=0, has_side_effects=True, vmem_limit_bytes=56 << 20
        ),
        name="main",
    )(img_emb, txt_feat, txt_head, log_scale, bias)


LAY = 96


def final_kernel(tiles_hbm, txt_hbm, img_hbm, head_out, txt_out, img_out, tiles, head, txt, img, sems):
    txt_in = pltpu.make_async_copy(txt_hbm, txt, sems.at[0])
    img_in = pltpu.make_async_copy(img_hbm, img, sems.at[1])
    txt_back = pltpu.make_async_copy(txt, txt_out, sems.at[2])
    img_back = pltpu.make_async_copy(img, img_out, sems.at[3])
    per = LAY // 16 * COLS
    blocks = HALF // LAY

    def read(i):
        at = pl.ds((i % blocks) * per, per)
        return pltpu.make_async_copy(tiles_hbm.at[i // blocks, at], tiles.at[i // blocks, at], sems.at[4 + i])

    def write(i):
        at = rows_at(i * LAY, LAY)
        return pltpu.make_async_copy(head.at[at], head_out.at[at], sems.at[4 + CS * blocks + i])

    each(0, CS * blocks, lambda i: read(i).start())
    txt_in.start()
    img_in.start()

    def lay(i):
        read(i).wait()
        for r in range(LAY // 16):
            for col in range(COLS):
                value = tiles[i // blocks, (i % blocks) * per + r * COLS + col]
                head[pl.ds(pl.multiple_of(i * LAY + r * 16, 16), 16), col * 128:(col + 1) * 128] = value.astype(F32)
        write(i).start()

    each(0, CS * blocks, lay)
    txt_in.wait()
    txt_back.start()
    img_in.wait()
    img_back.start()
    each(0, CS * blocks, lambda i: write(i).wait())
    txt_back.wait()
    img_back.wait()


def final_call(tiles, txt_grad, img_grad):
    return pl.pallas_call(
        final_kernel,
        out_shape=(
            jax.ShapeDtypeStruct((E, E), F32),
            jax.ShapeDtypeStruct((ROWS, E), BF16),
            jax.ShapeDtypeStruct((ROWS, E), BF16),
        ),
        in_specs=[pl.BlockSpec(memory_space=pl.ANY)] * 3,
        out_specs=[pl.BlockSpec(memory_space=pl.ANY)] * 3,
        scratch_shapes=[
            pltpu.VMEM((CS, NT, 16, 128), BF16),
            pltpu.VMEM((E, E), F32),
            pltpu.VMEM((ROWS, E), BF16),
            pltpu.VMEM((ROWS, E), BF16),
            pltpu.SemaphoreType.DMA((4 + 2 * CS * HALF // LAY,)),
        ],
        compiler_params=pltpu.CompilerParams(vmem_limit_bytes=56 << 20),
        name="final",
    )(tiles, txt_grad, img_grad)


def shards(img_emb, txt_feat, txt_head, log_scale, bias):
    tiles, txt_grad, img_grad = main_call(img_emb, txt_feat, txt_head, log_scale, bias)
    head_grad, txt_grad, img_grad = final_call(tiles, txt_grad, img_grad)
    return (img_grad, txt_grad, head_grad)


def solution(mesh):
    return jax.shard_map(
        shards,
        mesh=mesh,
        in_specs=(P("batch", None), P("batch", None), P(), P(), P()),
        out_specs=(P("batch", None), P("batch", None), P()),
        check_vma=False,
    )
```

time: 91.8 us -> 85 us (0.926)
  Pallas kernels: 89.7 us -> 82.9 us
    pallas_call x1, Pallas kernels: 84.2 us -> 77.5 us  [main_call(): pl.pallas_call(main_kernel, out_shape=(jax.ShapeDtypeStruct((CS, NT, 16,...]
where the time goes in v3:
time: 85 us; the launch traced here: 84.9 us
  Pallas kernels  82.9 us (98%)
  between operations  1.93 us (2%)
    pallas_call x1, Pallas kernels, main_call(): pl.pallas_call(main_kernel, out_shape=(jax.ShapeDtypeStruct((CS, NT, 16,...  77.5 us
    pallas_call x1, Pallas kernels, final_call(): pl.pallas_call(final_kernel, out_shape=(jax.ShapeDtypeStruct((E, E), F32)...  5.46 us

profile of v3, /device:TPU:1, one launch (start us, length us, event | category | flops | bytes accessed | tf_op | source)
XLA Modules:
  0.0 84.9 jit_solution(9460292268142262468)
XLA Ops:
  1.9 77.5 %main.1 = (bf16[2,328,16,128]{3,2,1,0:T(8,128)(2,1)}, bf16[512,1152]{1,0:T(8,128)(2,1)}, bf16[512,1152]{1,0:T(8,128)(2,1)}) custom-call(bf16[512,1152]{1,0:T(8,128)(2,1)} %img_hbm.1, bf16[512,1152]{1,0:T(8,128)(2,1)} %feat_hbm.1, bf16[1152,1152]{1,0:T(8,128)(2,1)} %head_hbm.1, f32[1]{0:T(128)S(6)} %copy.8.scale_ref, f32[1]{0:T(128)S(6)} %copy.9.bias_ref), custom_call_target="tpu_custom_call" | custom-call | tf_op jit(solution)/shard_map/main/pallas_call | solution.py:477
  79.4 5.5 %final.1 = (f32[1152,1152]{1,0:T(8,128)}, bf16[512,1152]{1,0:T(8,128)(2,1)}, bf16[512,1152]{1,0:T(8,128)(2,1)}) custom-call(bf16[2,328,16,128]{3,2,1,0:T(8,128)(2,1)} %get-tuple-element.9.tiles_hbm, bf16[512,1152]{1,0:T(8,128)(2,1)} %get-tuple-element.10.txt_hbm, bf16[512,1152]{1,0:T(8,128)(2,1)} %get-tuple-element.11.img_hbm), custom_call_target="tpu_custom_call" | custom-call | tf_op jit(solution)/shard_map/final/pallas_call | solution.py:536

commit v4 on v3

--- a/solution.py
+++ b/solution.py
@@ -212,7 +212,7 @@
 
 
 RC = 128
-EARLY = 256
+EARLY = 320
 NC = ROWS // RC
 CW = 384
 TAIL = 256
@@ -380,12 +380,12 @@
                 s.w[(i * HB // 16 + r) * COLS + col] = value[r * 16:(r + 1) * 16, col * 128:(col + 1) * 128]
 
     head_both(0)
+    a1.start_scatter()
     b1.start_scatter()
-    a1.start_scatter()
     head_both(1)
     s.w[UNITS * COLS:] = jnp.zeros((NT - UNITS * COLS, 16, 128), BF16)
+    a2.start_scatter()
     b2.start_scatter()
-    a2.start_scatter()
 
     txt_write = pltpu.make_async_copy(s.txt_grad, txt_out, s.outs.at[0])
     img_write = pltpu.make_async_copy(s.img_grad, img_out, s.outs.at[1])
@@ -491,7 +491,7 @@
     )(img_emb, txt_feat, txt_head, log_scale, bias)
 
 
-LAY = 96
+LAY = 288
 
 
 def final_kernel(tiles_hbm, txt_hbm, img_hbm, head_out, txt_out, img_out, tiles, head, txt, img, sems):

time: 85 us -> 83.6 us (0.984)
  Pallas kernels: 82.9 us -> 81.6 us
    pallas_call x1, Pallas kernels: 5.46 us -> 4.43 us  [final_call(): pl.pallas_call(final_kernel, out_shape=(jax.ShapeDtypeStruct((E, E), F32)...]
where the time goes in v4:
time: 83.6 us; the launch traced here: 83.5 us
  Pallas kernels  81.6 us (98%)
  between operations  1.93 us (2%)
    pallas_call x1, Pallas kernels, main_call(): pl.pallas_call(main_kernel, out_shape=(jax.ShapeDtypeStruct((CS, NT, 16,...  77.1 us
    pallas_call x1, Pallas kernels, final_call(): pl.pallas_call(final_kernel, out_shape=(jax.ShapeDtypeStruct((E, E), F32)...  4.43 us

profile of v4, /device:TPU:1, one launch (start us, length us, event | category | flops | bytes accessed | tf_op | source)
XLA Modules:
  0.0 83.5 jit_solution(7378236794291364782)
XLA Ops:
  1.9 77.1 %main.1 = (bf16[2,328,16,128]{3,2,1,0:T(8,128)(2,1)}, bf16[512,1152]{1,0:T(8,128)(2,1)}, bf16[512,1152]{1,0:T(8,128)(2,1)}) custom-call(bf16[512,1152]{1,0:T(8,128)(2,1)} %img_hbm.1, bf16[512,1152]{1,0:T(8,128)(2,1)} %feat_hbm.1, bf16[1152,1152]{1,0:T(8,128)(2,1)} %head_hbm.1, f32[1]{0:T(128)S(6)} %copy.8.scale_ref, f32[1]{0:T(128)S(6)} %copy.9.bias_ref), custom_call_target="tpu_custom_call" | custom-call | tf_op jit(solution)/shard_map/main/pallas_call | solution.py:477
  79.1 4.4 %final.1 = (f32[1152,1152]{1,0:T(8,128)}, bf16[512,1152]{1,0:T(8,128)(2,1)}, bf16[512,1152]{1,0:T(8,128)(2,1)}) custom-call(bf16[2,328,16,128]{3,2,1,0:T(8,128)(2,1)} %get-tuple-element.9.tiles_hbm, bf16[512,1152]{1,0:T(8,128)(2,1)} %get-tuple-element.10.txt_hbm, bf16[512,1152]{1,0:T(8,128)(2,1)} %get-tuple-element.11.img_hbm), custom_call_target="tpu_custom_call" | custom-call | tf_op jit(solution)/shard_map/final/pallas_call | solution.py:536

commit v5 on v4

--- a/solution.py
+++ b/solution.py
@@ -399,7 +399,9 @@
     s.wt[:, 0:ROWS] = weights(s.imgs[own, :], s.txts[own, :], True)
     txt_near.wait_recv()
     s.wt[:, ROWS:2 * ROWS] = weights(s.imgs[own, :], s.txts[nbr, :])
+    b1.start_scatter2()
     sums_of(s.img_sum, s.txts, 0, 2 * ROWS, False)
+    a1.start_scatter2()
 
     def image_far(j):
         start, size = ((0, EARLY), (EARLY, ROWS - EARLY))[j]
@@ -409,7 +411,7 @@
 
     image_far(0)
 
-    for line in (b1, a1, b2, a2):
+    for line in (b2, a2):
         line.start_scatter2()
     txt_far(1).start()
     for line in (b1, a1, b2, a2):

time: 83.6 us -> 85.8 us (1.026)
  Pallas kernels: 81.6 us -> 83.7 us
    pallas_call x1, Pallas kernels: 77.1 us -> 79.3 us  [main_call(): pl.pallas_call(main_kernel, out_shape=(jax.ShapeDtypeStruct((CS, NT, 16,...]
where the time goes in v5:
time: 85.8 us; the launch traced here: 85.7 us
  Pallas kernels  83.7 us (98%)
  between operations  1.93 us (2%)
    pallas_call x1, Pallas kernels, main_call(): pl.pallas_call(main_kernel, out_shape=(jax.ShapeDtypeStruct((CS, NT, 16,...  79.3 us
    pallas_call x1, Pallas kernels, final_call(): pl.pallas_call(final_kernel, out_shape=(jax.ShapeDtypeStruct((E, E), F32)...  4.43 us

profile of v5, /device:TPU:1, one launch (start us, length us, event | category | flops | bytes accessed | tf_op | source)
XLA Modules:
  0.0 85.7 jit_solution(3767160928819046884)
XLA Ops:
  1.9 79.3 %main.1 = (bf16[2,328,16,128]{3,2,1,0:T(8,128)(2,1)}, bf16[512,1152]{1,0:T(8,128)(2,1)}, bf16[512,1152]{1,0:T(8,128)(2,1)}) custom-call(bf16[512,1152]{1,0:T(8,128)(2,1)} %img_hbm.1, bf16[512,1152]{1,0:T(8,128)(2,1)} %feat_hbm.1, bf16[1152,1152]{1,0:T(8,128)(2,1)} %head_hbm.1, f32[1]{0:T(128)S(6)} %copy.8.scale_ref, f32[1]{0:T(128)S(6)} %copy.9.bias_ref), custom_call_target="tpu_custom_call" | custom-call | tf_op jit(solution)/shard_map/main/pallas_call | solution.py:479
  81.2 4.4 %final.1 = (f32[1152,1152]{1,0:T(8,128)}, bf16[512,1152]{1,0:T(8,128)(2,1)}, bf16[512,1152]{1,0:T(8,128)(2,1)}) custom-call(bf16[2,328,16,128]{3,2,1,0:T(8,128)(2,1)} %get-tuple-element.9.tiles_hbm, bf16[512,1152]{1,0:T(8,128)(2,1)} %get-tuple-element.10.txt_hbm, bf16[512,1152]{1,0:T(8,128)(2,1)} %get-tuple-element.11.img_hbm), custom_call_target="tpu_custom_call" | custom-call | tf_op jit(solution)/shard_map/final/pallas_call | solution.py:538
